TPU v7x, 512 devices: a whole 4x4x16 slice. The times are simulated.
512 devices in a mesh: energy: 32 (over z, core), transpor: 16 (over x, y).
Axes of the slice: x: 4, y: 4, z: 16, core: 2. Of those that a mesh axis runs over, the one named last changes fastest.
Arguments:
- energy_level: float32 [32], P('energy'), may hold values from -3 to 3
- sigma_real: float32 [32, 2048], P('energy', 'transpor'), may hold values from -1.5 to 1.5
- sigma_width: float32 [32, 2048], P('energy', 'transpor'), may hold values from 0.02 to 0.2
- onsite: float32 [16, 128, 128], P('transpor'), may hold values from -2 to 2, as said below
- coupling: float32 [16, 128, 128], P('transpor'), may hold values from -0.5 to 0.5
- source: float32 [2, 32, 16, 128, 128], P(None, 'energy', 'transpor'), may hold values from -6 to 6
- mode_strength: float32 [6], replicated, may hold values from 0.3 to 1.5
- mode_shift: int32 [6], replicated, may hold values from 1 to 10, as said below
Outputs:
- density: float32 [32, 2048], P('energy', 'transpor')
- sigma_phonon: float32 [32, 2048], P('energy', 'transpor')
Inputs may be any that keep to these rules, and one draw needn't show every extreme that they name: `mode_shift`: every value lies in 1 to 10, and at least one mode has exactly 10. `onsite`: each block is a symmetric matrix.
All inputs are finite; a program needn't handle non-finite values.
Results may differ from a plain program's by a relative error of at most 0.0003.
Values sent between devices are 32-bit elements; how exact they have to be, the bound alone decides.
No kernel may reach another device: no remote copies, remote signals or barrier semaphores. Data moves between devices by JAX's collectives and lax.ppermute only.
A program may use at most 64 MiB of HBM per device.

v0:
```python
import jax
import jax.numpy as jnp
from jax import lax
from jax.sharding import PartitionSpec as P

broadening = 0.2
highest = lax.Precision.HIGHEST


def from_behind(value, axis, steps):
    count = lax.axis_size(axis)
    leading, last = (max(0, -steps), min(count, count - steps))
    return lax.ppermute(value, axis, [(source, source + steps) for source in range(leading, last)])


def embed(real_part, imag_part):
    upper_half = jnp.concatenate([real_part, -imag_part], axis=-1)
    bottom = jnp.concatenate([imag_part, real_part], axis=-1)
    return jnp.concatenate([upper_half, bottom], axis=-2)


def batched(left_part, right_part):
    return jnp.einsum("enm,emk->enk", left_part, right_part, precision=highest)


def complex_product(left_part, right_part):
    real_out = batched(left_part[0], right_part[0]) - batched(left_part[1], right_part[1])
    imag_out = batched(left_part[0], right_part[1]) + batched(left_part[1], right_part[0])
    return jnp.stack([real_out, imag_out])


def cholesky_apply(factor, projected):
    return jax.scipy.linalg.cho_solve((factor, True), projected)


def complex_solve(diagonal, sources):
    orbitals = diagonal.shape[-1]
    system = embed(diagonal[0], diagonal[1])
    stacked = jnp.concatenate([sources[0], sources[1]], axis=-2)
    normal = jnp.einsum("eji,ejk->eik", system, system, precision=highest)
    factor = jnp.linalg.cholesky(normal)
    projected = jnp.einsum("eji,ejk->eik", system, stacked, precision=highest)
    result = jax.vmap(cholesky_apply)(factor, projected)
    return jnp.stack([result[:, :orbitals], result[:, orbitals:]])


def reduce_levels(diagonal, below_link, above_link, sources):
    orbitals = diagonal.shape[-1]
    levels = lax.axis_size("transpor").bit_length() - 1
    for depth_index in range(levels):
        stride = 1 << depth_index
        packed = complex_solve(
            diagonal, jnp.concatenate([below_link, above_link, sources], axis=-1)
        )
        from_left = from_behind(packed, "transpor", stride)
        from_right = from_behind(packed, "transpor", -stride)
        left_terms = complex_product(below_link, from_left)
        right_terms = complex_product(above_link, from_right)
        diagonal = diagonal - left_terms[..., orbitals : 2 * orbitals] - right_terms[..., :orbitals]
        below_link = -left_terms[..., :orbitals]
        above_link = -right_terms[..., orbitals : 2 * orbitals]
        sources = sources - left_terms[..., 2 * orbitals :] - right_terms[..., 2 * orbitals :]
    return complex_solve(diagonal, sources)


def phonon_weights(row_index, col_index, mode_strength, mode_shift):
    distance = col_index[None, :] - row_index[:, None]
    shifts = mode_shift[:, None, None]
    hits = (distance[None] == shifts).astype(jnp.float32) + (distance[None] == -shifts).astype(
        jnp.float32
    )
    return jnp.sum(mode_strength[:, None, None] * hits, axis=0)


def on_device(
    energy_level, sigma_real, sigma_width, onsite, coupling, source, mode_strength, mode_shift
):
    orbitals = onsite.shape[1]
    members = energy_level.shape[0]
    identity = jnp.eye(orbitals, dtype=jnp.float32)
    next_link = from_behind(coupling, "transpor", -1)[0]
    zero_block = jnp.zeros((members, orbitals, orbitals), jnp.float32)
    below_link = jnp.stack(
        [jnp.broadcast_to(-coupling[0].T, (members, orbitals, orbitals)), zero_block]
    )
    above_link = jnp.stack(
        [jnp.broadcast_to(-next_link, (members, orbitals, orbitals)), zero_block]
    )
    real_part = (energy_level[:, None] - sigma_real)[:, :, None] * identity - onsite[0]
    imag_part = (broadening + sigma_width)[:, :, None] * identity
    diagonal = jnp.stack([real_part, imag_part])
    sources = source[:, :, 0]
    solution = reduce_levels(diagonal, below_link, above_link, sources)
    density = jnp.mean(solution[0] ** 2 + solution[1] ** 2, axis=-1)
    owned = lax.all_to_all(density, "energy", split_axis=1, concat_axis=0, tiled=True)
    every_energy = jnp.arange(owned.shape[0], dtype=jnp.int32)
    weights = phonon_weights(every_energy, every_energy, mode_strength, mode_shift)
    mixed = jnp.dot(weights, owned, precision=highest)
    sigma_phonon = lax.all_to_all(mixed, "energy", split_axis=0, concat_axis=1, tiled=True)
    return (density, sigma_phonon)


def solution(mesh):
    placed = (
        P("energy"),
        P("energy", "transpor"),
        P("energy", "transpor"),
        P("transpor", None, None),
        P("transpor", None, None),
        P(None, "energy", "transpor", None, None),
        P(),
        P(),
    )
    return jax.shard_map(
        on_device,
        mesh=mesh,
        in_specs=placed,
        out_specs=(P("energy", "transpor"), P("energy", "transpor")),
        check_vma=False,
    )
```

profile of v0, /device:TPU:22, one launch (start us, length us, event | category | flops | bytes accessed | tf_op | source)
XLA Modules:
  0.0 467.1 jit_solution(17406097643662995832)
XLA Ops:
  0.6 1.0 copy.143
  1.6 2.4 collective-permute-start
  6.1 11.7 %custom-call.38 = f32[1,128,128]{2,1,0:T(8,128)S(1)} custom-call(f32[1,128,128]{2,1,0:T(8,128)S(1)} %cholesky.413), custom_call_target="Cholesky" | custom-call | tf_op jit(solution)/shard_map/jit(cholesky)/cholesky | solution.py:41
  17.9 9.8 %custom-call.39 = f32[1,1,128,128]{2,3,1,0:T(8,128)S(1)} custom-call(f32[1,1,128,128]{3,2,1,0:T(8,128)S(1)} %get-tuple-element.143), custom_call_target="InvertDiagBlocksLowerTriangular" | custom-call | tf_op jit(solution)/shard_map/jit(cholesky)/cholesky | solution.py:41
  28.2 11.7 %custom-call.40 = f32[1,128,128]{2,1,0:T(8,128)S(1)} custom-call(f32[1,128,128]{2,1,0:T(8,128)S(1)} %fusion.29), custom_call_target="Cholesky" | custom-call | tf_op jit(solution)/shard_map/jit(cholesky)/cholesky | solution.py:41
  41.9 4.2 while.10
  42.9 1.3 bitcast_dynamic-update-slice_fusion.16
  44.8 1.3 bitcast_dynamic-update-slice_fusion.16
  46.2 0.9 copy-done.1
  47.1 19.7 %custom-call.41 = f32[1,2,128,128]{2,3,1,0:T(8,128)S(1)} custom-call(f32[1,2,128,128]{3,2,1,0:T(8,128)S(1)} %bitcast.657), custom_call_target="InvertDiagBlocksLowerTriangular" | custom-call | tf_op jit(solution)/shard_map/vmap(jit(_cho_solve))/triangular_solve | solution.py:33
  69.6 2.4 collective-permute-start.2
  72.0 3.5 collective-permute-start.1
  75.6 6.6 %collective-permute-done.2 = f32[2,1,128,384]{3,2,1,0:T(8,128)S(1)} collective-permute-done((f32[2,1,128,384]{3,2,1,0:T(8,128)S(1)}, f32[2,1,128,384]{3,2,1,0:T(8,128)S(1)}, u32[]{:S(2)}, u32[]{:S(2)}) %collective-permute-start.2) | collective-permute-done | bytes 393248 | tf_op jit(solution)/shard_map/ppermute | solution.py:13
  83.1 2.7 collective-permute-done.1
  89.6 11.7 %custom-call.42 = f32[1,128,128]{2,1,0:T(8,128)S(1)} custom-call(f32[1,128,128]{2,1,0:T(8,128)S(1)} %cholesky.416), custom_call_target="Cholesky" | custom-call | tf_op jit(solution)/shard_map/jit(cholesky)/cholesky | solution.py:41
  101.3 9.8 %custom-call.43 = f32[1,1,128,128]{2,3,1,0:T(8,128)S(1)} custom-call(f32[1,1,128,128]{3,2,1,0:T(8,128)S(1)} %get-tuple-element.139), custom_call_target="InvertDiagBlocksLowerTriangular" | custom-call | tf_op jit(solution)/shard_map/jit(cholesky)/cholesky | solution.py:41
  111.6 24.7 %custom-call.44 = f32[1,128,128]{2,1,0:T(8,128)S(1)} custom-call(f32[1,128,128]{2,1,0:T(8,128)S(1)} %fusion.30), custom_call_target="Cholesky" | custom-call | tf_op jit(solution)/shard_map/jit(cholesky)/cholesky | solution.py:41
  136.4 0.7 compare_reduce_fusion.7
  139.0 4.1 while.11
  139.1 0.7 fusion.233
  139.7 1.3 bitcast_dynamic-update-slice_fusion.17
  141.8 1.3 bitcast_dynamic-update-slice_fusion.17
  143.1 19.7 %custom-call.45 = f32[1,2,128,128]{2,3,1,0:T(8,128)S(1)} custom-call(f32[1,2,128,128]{3,2,1,0:T(8,128)S(1)} %bitcast.658), custom_call_target="InvertDiagBlocksLowerTriangular" | custom-call | tf_op jit(solution)/shard_map/vmap(jit(_cho_solve))/triangular_solve | solution.py:33
  165.5 6.0 %collective-permute-start.4 = (f32[2,1,128,384]{3,2,1,0:T(8,128)S(1)}, f32[2,1,128,384]{3,2,1,0:T(8,128)S(1)}, u32[]{:S(2)}, u32[]{:S(2)}) collective-permute-start(f32[2,1,128,384]{3,2,1,0:T(8,128)S(1)} %pad_maximum_fusion.2), channel_id=1, source_target_pairs={{2,0},{3,1},{4,2},{5,3},{6,4},{7,5},{8,6},{9,7},{10,8},{11,9},{12,... | collective-permute-start | bytes 1179656 | tf_op jit(solution)/shard_map/ppermute | solution.py:13
  171.5 1.3 collective-permute-start.3
  172.8 14.0 %collective-permute-done.4 = f32[2,1,128,384]{3,2,1,0:T(8,128)S(1)} collective-permute-done((f32[2,1,128,384]{3,2,1,0:T(8,128)S(1)}, f32[2,1,128,384]{3,2,1,0:T(8,128)S(1)}, u32[]{:S(2)}, u32[]{:S(2)}) %collective-permute-start.4) | collective-permute-done | bytes 393248 | tf_op jit(solution)/shard_map/ppermute | solution.py:13
  191.6 11.7 %custom-call.46 = f32[1,128,128]{2,1,0:T(8,128)S(1)} custom-call(f32[1,128,128]{2,1,0:T(8,128)S(1)} %cholesky.419), custom_call_target="Cholesky" | custom-call | tf_op jit(solution)/shard_map/jit(cholesky)/cholesky | solution.py:41
  203.3 9.8 %custom-call.47 = f32[1,1,128,128]{2,3,1,0:T(8,128)S(1)} custom-call(f32[1,1,128,128]{3,2,1,0:T(8,128)S(1)} %get-tuple-element.135), custom_call_target="InvertDiagBlocksLowerTriangular" | custom-call | tf_op jit(solution)/shard_map/jit(cholesky)/cholesky | solution.py:41
  213.6 12.1 %custom-call.48 = f32[1,128,128]{2,1,0:T(8,128)S(1)} custom-call(f32[1,128,128]{2,1,0:T(8,128)S(1)} %fusion.31), custom_call_target="Cholesky" | custom-call | tf_op jit(solution)/shard_map/jit(cholesky)/cholesky | solution.py:41
  225.7 0.7 compare_reduce_fusion.5
  228.4 4.1 while.12
  229.1 1.3 bitcast_dynamic-update-slice_fusion.18
  231.1 1.3 bitcast_dynamic-update-slice_fusion.18
  232.5 19.7 %custom-call.49 = f32[1,2,128,128]{2,3,1,0:T(8,128)S(1)} custom-call(f32[1,2,128,128]{3,2,1,0:T(8,128)S(1)} %bitcast.659), custom_call_target="InvertDiagBlocksLowerTriangular" | custom-call | tf_op jit(solution)/shard_map/vmap(jit(_cho_solve))/triangular_solve | solution.py:33
  254.9 3.1 collective-permute-start.6
  258.0 1.5 collective-permute-start.5
  259.5 7.0 %collective-permute-done.6 = f32[2,1,128,384]{3,2,1,0:T(8,128)S(1)} collective-permute-done((f32[2,1,128,384]{3,2,1,0:T(8,128)S(1)}, f32[2,1,128,384]{3,2,1,0:T(8,128)S(1)}, u32[]{:S(2)}, u32[]{:S(2)}) %collective-permute-start.6) | collective-permute-done | bytes 393248 | tf_op jit(solution)/shard_map/ppermute | solution.py:13
  267.5 3.1 collective-permute-done.5
  274.5 11.7 %custom-call.50 = f32[1,128,128]{2,1,0:T(8,128)S(1)} custom-call(f32[1,128,128]{2,1,0:T(8,128)S(1)} %cholesky.422), custom_call_target="Cholesky" | custom-call | tf_op jit(solution)/shard_map/jit(cholesky)/cholesky | solution.py:41
  286.2 9.8 %custom-call.51 = f32[1,1,128,128]{2,3,1,0:T(8,128)S(1)} custom-call(f32[1,1,128,128]{3,2,1,0:T(8,128)S(1)} %get-tuple-element.131), custom_call_target="InvertDiagBlocksLowerTriangular" | custom-call | tf_op jit(solution)/shard_map/jit(cholesky)/cholesky | solution.py:41
  296.5 12.1 %custom-call.52 = f32[1,128,128]{2,1,0:T(8,128)S(1)} custom-call(f32[1,128,128]{2,1,0:T(8,128)S(1)} %fusion.32), custom_call_target="Cholesky" | custom-call | tf_op jit(solution)/shard_map/jit(cholesky)/cholesky | solution.py:41
  308.6 0.7 compare_reduce_fusion.3
  311.3 4.1 while.13
  312.0 1.3 bitcast_dynamic-update-slice_fusion.19
  313.4 0.7 fusion.235
  314.1 1.3 bitcast_dynamic-update-slice_fusion.19
  315.4 19.7 %custom-call.53 = f32[1,2,128,128]{2,3,1,0:T(8,128)S(1)} custom-call(f32[1,2,128,128]{3,2,1,0:T(8,128)S(1)} %bitcast.660), custom_call_target="InvertDiagBlocksLowerTriangular" | custom-call | tf_op jit(solution)/shard_map/vmap(jit(_cho_solve))/triangular_solve | solution.py:33
  337.8 2.8 collective-permute-start.8
  340.6 1.3 collective-permute-start.7
  341.9 6.3 %collective-permute-done.8 = f32[2,1,128,384]{3,2,1,0:T(8,128)S(1)} collective-permute-done((f32[2,1,128,384]{3,2,1,0:T(8,128)S(1)}, f32[2,1,128,384]{3,2,1,0:T(8,128)S(1)}, u32[]{:S(2)}, u32[]{:S(2)}) %collective-permute-start.8) | collective-permute-done | bytes 393248 | tf_op jit(solution)/shard_map/ppermute | solution.py:13
  349.3 4.7 %collective-permute-done.7 = f32[2,1,128,384]{3,2,1,0:T(8,128)S(1)} collective-permute-done((f32[2,1,128,384]{3,2,1,0:T(8,128)S(1)}, f32[2,1,128,384]{3,2,1,0:T(8,128)S(1)}, u32[]{:S(2)}, u32[]{:S(2)}) %collective-permute-start.7) | collective-permute-done | bytes 393248 | tf_op jit(solution)/shard_map/ppermute | solution.py:13
  357.7 11.7 %custom-call.54 = f32[1,128,128]{2,1,0:T(8,128)S(1)} custom-call(f32[1,128,128]{2,1,0:T(8,128)S(1)} %cholesky.425), custom_call_target="Cholesky" | custom-call | tf_op jit(solution)/shard_map/jit(cholesky)/cholesky | solution.py:41
  369.4 9.8 %custom-call.55 = f32[1,1,128,128]{2,3,1,0:T(8,128)S(1)} custom-call(f32[1,1,128,128]{3,2,1,0:T(8,128)S(1)} %get-tuple-element.127), custom_call_target="InvertDiagBlocksLowerTriangular" | custom-call | tf_op jit(solution)/shard_map/jit(cholesky)/cholesky | solution.py:41
  379.7 11.9 %custom-call.56 = f32[1,128,128]{2,1,0:T(8,128)S(1)} custom-call(f32[1,128,128]{2,1,0:T(8,128)S(1)} %fusion.33), custom_call_target="Cholesky" | custom-call | tf_op jit(solution)/shard_map/jit(cholesky)/cholesky | solution.py:41
  392.3 0.7 compare_reduce_fusion
  394.4 4.1 while.9
  395.0 1.4 bitcast_dynamic-update-slice_fusion.15
  397.1 1.4 bitcast_dynamic-update-slice_fusion.15
  398.5 19.7 %custom-call.22 = f32[1,2,128,128]{2,3,1,0:T(8,128)S(1)} custom-call(f32[1,2,128,128]{3,2,1,0:T(8,128)S(1)} %bitcast.656), custom_call_target="InvertDiagBlocksLowerTriangular" | custom-call | tf_op jit(solution)/shard_map/vmap(jit(_cho_solve))/triangular_solve | solution.py:33
  420.8 0.7 div.19
  421.5 15.6 %all-to-all-start = ((f32[1,32,4]{2,0,1:T(1,128)}), f32[1,32,4]{2,0,1:T(1,128)S(1)}, u32[]{:S(2)}, u32[]{:S(2)}) async-start(f32[1,32,4]{2,0,1:T(1,128)} %bitcast.178), calls=%async_computation | async-start | bytes 32768 | tf_op jit(solution)/shard_map/all_to_all | solution.py:95
  437.2 12.3 %all-to-all-done = f32[1,32,4]{2,0,1:T(1,128)S(1)} async-done(((f32[1,32,4]{2,0,1:T(1,128)}), f32[1,32,4]{2,0,1:T(1,128)S(1)}, u32[]{:S(2)}, u32[]{:S(2)}) %all-to-all-start) | async-done | bytes 544 | tf_op jit(solution)/shard_map/all_to_all | solution.py:95
  449.7 15.4 %all_to_all.29 = f32[32,1,4]{2,1,0:T(1,128)S(1)} all-to-all(f32[32,1,4]{2,1,0:T(1,128)S(1)} %bitcast.662), channel_id=1, replica_groups=mesh['energy'=32,'transpor'=16] {'energy'}, dimensions={0} | all-to-all | bytes 1024 | tf_op jit(solution)/shard_map/all_to_all | solution.py:99
  465.6 0.7 reduce.19
  (204 shorter events, 46.0 us)
Async XLA Ops:
  0.6 3.4 copy-start.2
  1.6 65.2 %collective-permute-start = (f32[1,128,128]{1,2,0:T(8,128)S(1)}, f32[1,128,128]{1,2,0:T(8,128)S(1)}, u32[]{:S(2)}, u32[]{:S(2)}) collective-permute-start(f32[1,128,128]{1,2,0:T(8,128)S(1)} %copy.143), channel_id=1, source_target_pairs={{1,0},{2,1},{3,2},{4,3},{5,4},{6,5},{7,6},{8,7},{9,8},{10,9},{11,1... | collective-permute-start | bytes 196616 | tf_op jit(solution)/shard_map/ppermute | solution.py:13
  4.1 0.7 copy-start.5
  4.8 0.7 copy-start.6
  41.9 4.2 copy-start
  46.1 0.9 copy-start.1
  69.6 12.5 %collective-permute-start.2 = (f32[2,1,128,384]{3,2,1,0:T(8,128)S(1)}, f32[2,1,128,384]{3,2,1,0:T(8,128)S(1)}, u32[]{:S(2)}, u32[]{:S(2)}) collective-permute-start(f32[2,1,128,384]{3,2,1,0:T(8,128)S(1)} %pad_maximum_fusion), channel_id=1, source_target_pairs={{1,0},{2,1},{3,2},{4,3},{5,4},{6,5},{7,6},{8,7},{9,8},{10,9},{11,1... | collective-permute-start | bytes 1179656 | tf_op jit(solution)/shard_map/ppermute | solution.py:13
  72.0 13.7 %collective-permute-start.1 = (f32[2,1,128,384]{3,2,1,0:T(8,128)S(1)}, f32[2,1,128,384]{3,2,1,0:T(8,128)S(1)}, u32[]{:S(2)}, u32[]{:S(2)}) collective-permute-start(f32[2,1,128,384]{3,2,1,0:T(8,128)S(1)} %pad_maximum_fusion), channel_id=1, source_target_pairs={{0,1},{1,2},{2,3},{3,4},{4,5},{5,6},{6,7},{7,8},{8,9},{9,10},{10,1... | collective-permute-start | bytes 1179656 | tf_op jit(solution)/shard_map/ppermute | solution.py:13
  165.5 21.2 %collective-permute-start.4 = (f32[2,1,128,384]{3,2,1,0:T(8,128)S(1)}, f32[2,1,128,384]{3,2,1,0:T(8,128)S(1)}, u32[]{:S(2)}, u32[]{:S(2)}) collective-permute-start(f32[2,1,128,384]{3,2,1,0:T(8,128)S(1)} %pad_maximum_fusion.2), channel_id=1, source_target_pairs={{2,0},{3,1},{4,2},{5,3},{6,4},{7,5},{8,6},{9,7},{10,8},{11,9},{12,... | collective-permute-start | bytes 1179656 | tf_op jit(solution)/shard_map/ppermute | solution.py:13
  171.5 16.3 %collective-permute-start.3 = (f32[2,1,128,384]{3,2,1,0:T(8,128)S(1)}, f32[2,1,128,384]{3,2,1,0:T(8,128)S(1)}, u32[]{:S(2)}, u32[]{:S(2)}) collective-permute-start(f32[2,1,128,384]{3,2,1,0:T(8,128)S(1)} %pad_maximum_fusion.2), channel_id=1, source_target_pairs={{0,2},{1,3},{2,4},{3,5},{4,6},{5,7},{6,8},{7,9},{8,10},{9,11},{10,... | collective-permute-start | bytes 1179656 | tf_op jit(solution)/shard_map/ppermute | solution.py:13
  254.9 11.6 %collective-permute-start.6 = (f32[2,1,128,384]{3,2,1,0:T(8,128)S(1)}, f32[2,1,128,384]{3,2,1,0:T(8,128)S(1)}, u32[]{:S(2)}, u32[]{:S(2)}) collective-permute-start(f32[2,1,128,384]{3,2,1,0:T(8,128)S(1)} %pad_maximum_fusion.4), channel_id=1, source_target_pairs={{4,0},{5,1},{6,2},{7,3},{8,4},{9,5},{10,6},{11,7},{12,8},{13,9},{1... | collective-permute-start | bytes 1179656 | tf_op jit(solution)/shard_map/ppermute | solution.py:13
  258.0 12.6 %collective-permute-start.5 = (f32[2,1,128,384]{3,2,1,0:T(8,128)S(1)}, f32[2,1,128,384]{3,2,1,0:T(8,128)S(1)}, u32[]{:S(2)}, u32[]{:S(2)}) collective-permute-start(f32[2,1,128,384]{3,2,1,0:T(8,128)S(1)} %pad_maximum_fusion.4), channel_id=1, source_target_pairs={{0,4},{1,5},{2,6},{3,7},{4,8},{5,9},{6,10},{7,11},{8,12},{9,13},{1... | collective-permute-start | bytes 1179656 | tf_op jit(solution)/shard_map/ppermute | solution.py:13
  337.8 2.8 copy-start.4
  337.8 10.5 %collective-permute-start.8 = (f32[2,1,128,384]{3,2,1,0:T(8,128)S(1)}, f32[2,1,128,384]{3,2,1,0:T(8,128)S(1)}, u32[]{:S(2)}, u32[]{:S(2)}) collective-permute-start(f32[2,1,128,384]{3,2,1,0:T(8,128)S(1)} %pad_maximum_fusion.6), channel_id=1, source_target_pairs={{8,0},{9,1},{10,2},{11,3},{12,4},{13,5},{14,6},{15,7},{24,16},{25,... | collective-permute-start | bytes 1179656 | tf_op jit(solution)/shard_map/ppermute | solution.py:13
  340.6 13.3 %collective-permute-start.7 = (f32[2,1,128,384]{3,2,1,0:T(8,128)S(1)}, f32[2,1,128,384]{3,2,1,0:T(8,128)S(1)}, u32[]{:S(2)}, u32[]{:S(2)}) collective-permute-start(f32[2,1,128,384]{3,2,1,0:T(8,128)S(1)} %pad_maximum_fusion.6), channel_id=1, source_target_pairs={{0,8},{1,9},{2,10},{3,11},{4,12},{5,13},{6,14},{7,15},{16,24},{17,... | collective-permute-start | bytes 1179656 | tf_op jit(solution)/shard_map/ppermute | solution.py:13
  421.5 15.6 %copy-start.3 = (f32[6]{0:T(128)S(1)}, f32[6]{0:T(128)}, u32[]{:S(2)}) copy-start(f32[6]{0:T(128)} %param.17) | copy-start | bytes 76
  421.5 28.0 %all-to-all-start = ((f32[1,32,4]{2,0,1:T(1,128)}), f32[1,32,4]{2,0,1:T(1,128)S(1)}, u32[]{:S(2)}, u32[]{:S(2)}) async-start(f32[1,32,4]{2,0,1:T(1,128)} %bitcast.178), calls=%async_computation | async-start | bytes 32768 | tf_op jit(solution)/shard_map/all_to_all | solution.py:95
where the time goes:
time: 476 us; the launch traced here: 467 us
  other arithmetic  287 us (60%)
  waiting for transfers between devices  56.7 us (12%)
  starting transfers between devices  39.7 us (8%)
  matrix products  32.8 us (7%)
  local copies, waits for them, and re-layouts  25.5 us (5%)
  blocking collectives  15.4 us (3%)
  between operations  9.22 us (2%)
    another operation x34, other arithmetic, complex_solve(): factor = jnp.linalg.cholesky(normal)  186 us
    another operation x11, other arithmetic, cholesky_apply(): return jax.scipy.linalg.cho_solve((factor, True), projected)  98.5 us
    ppermute x9, waiting for transfers between devices, from_behind(): lax.ppermute(value, axis, [(source, source + steps) for source in range(l...  44.4 us
    ppermute x9, starting transfers between devices, from_behind(): lax.ppermute(value, axis, [(source, source + steps) for source in range(l...  24.1 us
    another operation x30, local copies, waits for them, and re-layouts, cholesky_apply(): return jax.scipy.linalg.cho_solve((factor, True), projected)  16 us
    dot_general x32, matrix products, batched(): return jnp.einsum('enm,emk->enk', left_part, right_part, precision=highest)  15.7 us
    all_to_all x1, starting transfers between devices, on_device(): lax.all_to_all(density, 'energy', split_axis=1, concat_axis=0, tiled=True)  15.6 us
    all_to_all x1, blocking collectives, on_device(): lax.all_to_all(mixed, 'energy', split_axis=0, concat_axis=1, tiled=True)  15.4 us
  transfers between devices with their start and end apart: 10, of which 8 were waited for; matrix products, arithmetic and copies ran while one was open for 13% of the time, Pallas kernels for 0%

commit v1 on v0

v1 whole, which is shorter than its diff:
```python
import functools

import jax
import jax.numpy as jnp
from jax import lax
from jax.experimental import pallas as pl
from jax.experimental.pallas import tpu as pltpu
from jax.sharding import PartitionSpec as P

N = 128
TILES = N // 8
HALF = 8
COLS = 16
PACK = N + 8
broadening = 0.2
prec = lax.Precision.HIGHEST
f32 = jnp.float32

GROUPS = [list(range(8)), [12, 13, 14, 15, 8, 9, 10, 11]]
MIRROR = [(x * 4 + y, (3 - x) * 4 + y) for x in range(4) for y in range(4)]


def dot(a, b, dims=((1,), (0,))):
    return lax.dot_general(a, b, (dims, ((), ())), precision=prec, preferred_element_type=f32)


def lanes_of(v, k):
    return jnp.broadcast_to(v[:, k : k + 1], (8, N))


def row_of(v, k):
    return jnp.broadcast_to(v[k : k + 1, :], (8, N))


def pack(re, im):
    return jnp.concatenate([re, im], axis=1)


def turned(v):
    return pack(-v[:, N:], v[:, :N])


def rows_for(v):
    return jnp.concatenate([v, turned(v)], axis=0)


def flip(v):
    return pack(v[:, :N].T, v[:, N:].T)


def times(a, b):
    return dot(a, rows_for(b))


def times_t(a, b):
    f = jnp.concatenate([pack(b[:, :N], -b[:, N:]), pack(b[:, N:], b[:, :N])], axis=0)
    return dot(a, f, ((1,), (1,)))


def iota(shape, d):
    return lax.broadcasted_iota(jnp.int32, shape, d)


def invert(ms, ahead=2):
    R = [[m[8 * u : 8 * u + 8, :N] for u in range(TILES)] for m in ms]
    I = [[m[8 * u : 8 * u + 8, N:] for u in range(TILES)] for m in ms]
    sub, lane = iota((8, N), 0), iota((8, N), 1)
    zero = jnp.zeros((8, 2 * N), f32)
    for t in range(TILES):
        here = (lane >= 8 * t) & (lane < 8 * t + 8)
        unit = jnp.where(lane == sub + 8 * t, 1.0, 0.0)
        for b in range(len(ms)):
            xr, xi = R[b], I[b]
            dr = [lanes_of(xr[t], 8 * t + j) for j in range(8)]
            di = [lanes_of(xi[t], 8 * t + j) for j in range(8)]
            soon = range(t + 1, min(t + 1 + ahead, TILES))
            lr = {u: [lanes_of(xr[u], 8 * t + j) for j in range(8)] for u in soon}
            li = {u: [lanes_of(xi[u], 8 * t + j) for j in range(8)] for u in soon}
            pr = jnp.where(here, unit, xr[t])
            pi = jnp.where(here, 0.0, xi[t])
            for k in range(8):
                p_r, p_i = row_of(dr[k], k), row_of(di[k], k)
                scale = 1.0 / (p_r * p_r + p_i * p_i)
                ir, ii = p_r * scale, p_i * scale
                cr = dr[k] - jnp.where(sub == k, 1.0, 0.0)
                ci = di[k]
                fr = cr * ir + ci * ii
                fi = ci * ir - cr * ii
                for j in range(k + 1, 8):
                    br, bi = row_of(dr[j], k), row_of(di[j], k)
                    dr[j] = dr[j] - fr * br + fi * bi
                    di[j] = di[j] - fr * bi - fi * br
                br, bi = row_of(pr, k), row_of(pi, k)
                pr = pr - fr * br + fi * bi
                pi = pi - fr * bi - fi * br
            new = {t: (pr, pi)}
            for u in soon:
                yr = jnp.where(here, 0.0, xr[u])
                yi = jnp.where(here, 0.0, xi[u])
                for j in range(8):
                    br, bi = row_of(pr, j), row_of(pi, j)
                    yr = yr - lr[u][j] * br + li[u][j] * bi
                    yi = yi - lr[u][j] * bi - li[u][j] * br
                new[u] = (yr, yi)
            rest = [u for u in range(TILES) if u not in new]
            left = jnp.concatenate([pack(xr[u], xi[u]) for u in rest], 0)
            top = [pack(pr, pi) if u == t else zero for u in range(TILES)]
            low = [pack(-pi, pr) if u == t else zero for u in range(TILES)]
            delta = dot(left, jnp.concatenate(top + low, 0))
            for q, u in enumerate(rest):
                new[u] = (
                    jnp.where(here, 0.0, xr[u]) - delta[8 * q : 8 * q + 8, :N],
                    jnp.where(here, 0.0, xi[u]) - delta[8 * q : 8 * q + 8, N:],
                )
            R[b] = [new[u][0] for u in range(TILES)]
            I[b] = [new[u][1] for u in range(TILES)]
    return [jnp.concatenate([pack(r, i) for r, i in zip(R[b], I[b])], 0) for b in range(len(ms))]


def fold(m):
    re, im = m[:, :N], m[:, N:]
    i, j = iota((N, N), 0), iota((N, N), 1)
    diagonal = jnp.sum(jnp.where(i == j, im, 0.0), axis=0, keepdims=True)
    return jnp.concatenate([jnp.where(i >= j, re, im), jnp.broadcast_to(diagonal, (8, N))], axis=0)


def unfold(v):
    a, diagonal = v[:N], v[N : N + 1]
    i, j = iota((N, N), 0), iota((N, N), 1)
    at = a.T
    re = jnp.where(i >= j, a, at)
    im = jnp.where(i == j, diagonal, jnp.where(i < j, a, at))
    return pack(re, im)


def prepare_kernel(side_ref, coupling_ref, source_ref, coupling_out, source_out):
    link = coupling_ref[0]
    coupling_out[...] = jnp.where(side_ref[0] == 1, link.T, link)
    for part in range(2):
        flipped = source_ref[part, 0, 0].T
        for q in range(HALF):
            source_out[q, COLS * part : COLS * (part + 1)] = flipped[COLS * q : COLS * (q + 1)]


def own_kernel(side_ref, energy_ref, shift_ref, width_ref, onsite_ref, out_ref):
    i, j = iota((N, N), 0), iota((N, N), 1)
    re = jnp.where(i == j, energy_ref[0] - shift_ref[...], 0.0) - onsite_ref[0]
    im = jnp.where(i == j, broadening + width_ref[...], 0.0)
    block = pack(re, im)

    @pl.when(side_ref[1] == 0)
    def _():
        out_ref[...] = fold(invert([block])[0])

    @pl.when(side_ref[1] == 1)
    def _():
        out_ref[...] = fold(block)


def half_kernel(side_ref, blocks_ref, first_ref, mid_ref, w_ref, y_ref):
    right = side_ref[0]
    place = [jnp.bitwise_xor(m, 3 * right) for m in range(HALF)]
    link_place = [jnp.where(right == 1, place[m], m + 1) for m in range(HALF - 1)]
    U = [first_ref[link_place[m], :N] for m in range(HALF - 1)]
    blocks = [unfold(blocks_ref[place[m]]) for m in range(HALF)]
    z = [pack(first_ref[place[m], N : N + COLS], first_ref[place[m], N + COLS :]) for m in range(HALF)]
    D = {m: blocks[m] for m in range(1, HALF, 2)}
    UT = [u.T for u in U]
    V = {}
    slot = iter(range(11))

    def keep(w):
        w_ref[next(slot)] = w

    for m in range(0, HALF, 2):
        p = blocks[m]
        stacked = jnp.concatenate([p[:, :N], p[:, N:]], axis=0)
        y_ref[m] = times(z[m], p)
        if m == 0:
            w = dot(stacked, U[0])
            wr = pack(w[:N], w[N:])
        else:
            w = dot(stacked, pack(UT[m - 1], U[m]))
            wl = pack(w[:N, :N], w[N:, :N])
            wr = pack(w[:N, N:], w[N:, N:])
            up = dot(U[m - 1], jnp.concatenate([wl, wr], axis=1))
            D[m - 1] = D[m - 1] - up[:, : 2 * N]
            V[m - 1] = up[:, 2 * N :]
            z[m - 1] = z[m - 1] + times(z[m], wl)
            keep(wl)
        D[m + 1] = D[m + 1] - dot(UT[m], wr)
        z[m + 1] = z[m + 1] + times(z[m], wr)
        keep(wr)

    p1, p5 = invert([D[1], D[5]])
    y_ref[1] = times(z[1], p1)
    y_ref[5] = times(z[5], p5)
    w1r = times(p1, V[1])
    w5l = times(p5, flip(V[3]))
    w5r = times(p5, V[5])
    D[3] = D[3] - times(flip(V[1]), w1r) - times(V[3], w5l)
    V3 = times(V[3], w5r)
    D[7] = D[7] - times(flip(V[5]), w5r)
    z[3] = z[3] + times(z[1], w1r) + times(z[5], w5l)
    z[7] = z[7] + times(z[5], w5r)
    keep(w1r)
    keep(w5l)
    keep(w5r)

    (p3,) = invert([D[3]])
    y_ref[3] = times(z[3], p3)
    w3r = times(p3, V3)
    keep(w3r)
    D[7] = D[7] - times(flip(V3), w3r)
    z[7] = z[7] + times(z[3], w3r)
    mid_ref[:PACK] = fold(D[7])
    mid_ref[PACK : PACK + COLS] = z[7][:, :N]
    mid_ref[PACK + COLS :] = z[7][:, N:]


def middle_kernel(side_ref, mine_ref, other_ref, own_link_ref, sent_link_ref, w_ref, y_ref, out_ref):
    right = side_ref[0]
    sent = sent_link_ref[...]
    U = jnp.where(right == 1, own_link_ref[...], sent.T)
    UT = jnp.where(right == 1, own_link_ref[...].T, sent)
    mine = unfold(mine_ref[:PACK])
    z = pack(mine_ref[PACK : PACK + COLS], mine_ref[PACK + COLS :])
    z_other = pack(other_ref[PACK : PACK + COLS], other_ref[PACK + COLS :])
    (q,) = invert([unfold(other_ref[:PACK])])
    w = dot(jnp.concatenate([q[:, :N], q[:, N:]], axis=0), UT)
    w = pack(w[:N], w[N:])
    z = z + times(z_other, w)
    (s,) = invert([mine - dot(U, w)])
    x = {7: times(z, s)}
    x[3] = y_ref[3] + times_t(x[7], w_ref[10])
    x[5] = y_ref[5] + times_t(x[3], w_ref[8]) + times_t(x[7], w_ref[9])
    x[1] = y_ref[1] + times_t(x[3], w_ref[7])
    x[0] = y_ref[0] + times_t(x[1], w_ref[0])
    for m in (2, 4, 6):
        x[m] = y_ref[m] + times_t(x[m - 1], w_ref[m - 1]) + times_t(x[m + 1], w_ref[m])
    for m in range(HALF):
        squares = x[m] * x[m]
        total = jnp.sum(squares[:, :N] + squares[:, N:], axis=0, keepdims=True) * (1.0 / N)
        out_ref[jnp.bitwise_xor(m, 3 * right)] = total[0]


def call(kernel, shapes, smem, operands, name):
    vmem = pl.BlockSpec(memory_space=pltpu.VMEM)
    scalar = pl.BlockSpec(memory_space=pltpu.SMEM)
    many = isinstance(shapes, list)
    return pl.pallas_call(
        kernel,
        out_shape=[jax.ShapeDtypeStruct(s, f32) for s in shapes] if many else jax.ShapeDtypeStruct(shapes, f32),
        in_specs=[scalar] * smem + [vmem] * (len(operands) - smem),
        out_specs=[vmem] * len(shapes) if many else vmem,
        compiler_params=pltpu.CompilerParams(vmem_limit_bytes=40 * 2**20),
        name=name,
    )(*operands)


def on_device(energy_level, sigma_real, sigma_width, onsite, coupling, source, mode_strength, mode_shift):
    place = lax.axis_index("transpor")
    right = (place >= HALF).astype(jnp.int32)
    odd = jnp.bitwise_xor(place % 2, right)
    side = jnp.stack([right, odd])
    exchange = functools.partial(
        lax.all_to_all, axis_name="transpor", split_axis=0, concat_axis=0, axis_index_groups=GROUPS, tiled=True
    )

    link, columns = call(prepare_kernel, [(N, N), (HALF, 2 * COLS, N)], 1, (side, coupling, source), "prepare")
    first = exchange(jnp.concatenate([jnp.broadcast_to(link, (HALF, N, N)), columns], axis=1))
    own = call(own_kernel, (PACK, N), 2, (side, energy_level, sigma_real, sigma_width, onsite), "own_inverse")
    blocks = exchange(jnp.broadcast_to(own, (HALF, PACK, N)))
    middle, w, y = call(
        half_kernel,
        [(PACK + 2 * COLS, N), (11, N, 2 * N), (HALF, COLS, 2 * N)],
        1,
        (side, blocks, first),
        "half",
    )
    own_link = first[4, :N]
    sent_link = lax.ppermute(own_link, "transpor", MIRROR)
    other = lax.ppermute(middle, "transpor", MIRROR)
    sums = call(middle_kernel, (HALF, N), 1, (side, middle, other, own_link, sent_link, w, y), "middle")
    density = jnp.sum(exchange(sums), axis=0, keepdims=True)
    return (density, mix(density, mode_strength, mode_shift))


def mix(density, mode_strength, mode_shift):
    energies = lax.axis_size("energy")
    index = lax.axis_index("energy")
    odd = index % 2
    couples = [[e, e + 1] for e in range(0, energies, 2)]

    def fetch(value, chips):
        steps = [(e, e - 2 * chips if e % 2 == 0 else e + 2 * chips) for e in range(energies)]
        return lax.ppermute(value, "energy", [(a, b) for a, b in steps if 0 <= b < energies])

    own = lax.all_gather(density, "energy", axis_index_groups=couples, tiled=True)
    near = jnp.concatenate([own, fetch(own, 1)], axis=0)
    middle = fetch(near, 2)
    far = fetch(middle, 2)
    window = jnp.concatenate([near, middle, far], axis=0)
    row = jnp.arange(window.shape[0], dtype=jnp.int32)
    chip = row // 2
    offset = jnp.where(odd == 1, -chip, chip) * 2 + row % 2
    used = jnp.where((odd == 1) & (chip == 0), 0.0, 1.0)
    target = jnp.arange(2, dtype=jnp.int32)
    distance = jnp.abs(offset[None, :] - target[:, None])
    hits = (distance[None] == mode_shift[:, None, None]).astype(f32)
    weights = jnp.sum(mode_strength[:, None, None] * hits, axis=0) * used
    partial = jnp.sum(weights[:, :, None] * window[None], axis=1)
    both = lax.all_gather(partial, "energy", axis_index_groups=couples)
    return lax.dynamic_slice_in_dim(both[0] + both[1], odd, 1, axis=0)


def solution(mesh):
    placed = (
        P("energy"),
        P("energy", "transpor"),
        P("energy", "transpor"),
        P("transpor", None, None),
        P("transpor", None, None),
        P(None, "energy", "transpor", None, None),
        P(),
        P(),
    )
    return jax.shard_map(
        on_device,
        mesh=mesh,
        in_specs=placed,
        out_specs=(P("energy", "transpor"), P("energy", "transpor")),
        check_vma=False,
    )
```

time: 476 us -> 120 us (0.25)
  the two profiles are of different devices: /device:TPU:22 before, /device:TPU:1 now
where the time goes in v1:
time: 120 us; the launch traced here: 118 us
  Pallas kernels  39 us (32%)
  starting transfers between devices  38.4 us (32%)
  waiting for transfers between devices  24.3 us (20%)
  blocking collectives  10.2 us (8%)
  local copies, waits for them, and re-layouts  3.67 us (3%)
  between operations  1.54 us (1%)
  other arithmetic  1.21 us (1%)
    pallas_call x4, Pallas kernels, call(): pl.pallas_call(kernel, out_shape=[jax.ShapeDtypeStruct(s, f32) for s in s...  39 us
    ppermute x3, starting transfers between devices, fetch(): lax.ppermute(value, 'energy', [(a, b) for a, b in steps if 0 <= b < energ...  15.8 us
    ppermute x1, starting transfers between devices, on_device(): other = lax.ppermute(middle, 'transpor', MIRROR)  7.72 us
    all_to_all x1, waiting for transfers between devices, on_device(): exchange(jnp.concatenate([jnp.broadcast_to(link, (HALF, N, N)), columns],...  7.37 us
    all_gather x1, blocking collectives, mix(): lax.all_gather(density, 'energy', axis_index_groups=couples, tiled=True)  6.25 us
    all_to_all x1, starting transfers between devices, on_device(): blocks = exchange(jnp.broadcast_to(own, (HALF, PACK, N)))  5.95 us
    all_to_all x1, waiting for transfers between devices, on_device(): blocks = exchange(jnp.broadcast_to(own, (HALF, PACK, N)))  5.64 us
    all_to_all x1, waiting for transfers between devices, on_device(): density = jnp.sum(exchange(sums), axis=0, keepdims=True)  4.77 us
  transfers between devices with their start and end apart: 8, of which 7 were waited for; matrix products, arithmetic and copies ran while one was open for 1% of the time, Pallas kernels for 1%

profile of v1, /device:TPU:1, one launch (start us, length us, event | category | flops | bytes accessed | tf_op | source)
XLA Modules:
  0.0 118.3 jit_solution(7299684376875696414)
XLA Ops:
  0.6 0.0 copy-start.1
  0.6 0.0 copy-start
  1.3 0.1 pad_add_fusion.side_ref
  1.4 0.0 copy-start.2
  1.4 0.8 copy-done.2
  2.3 0.0 copy-start.3
  2.3 0.7 copy-done.3
  2.9 0.0 copy-start.4
  2.9 0.7 copy-done.4
  3.6 5.4 %own_inverse.1 = f32[136,128]{1,0:T(8,128)S(1)} custom-call(s32[2]{0:T(128)S(1)} %pad_add_fusion.side_ref, f32[1]{0:T(128)S(6)} %copy.13.energy_ref, f32[1,128]{1,0:T(1,128)S(1)} %copy-done.3, f32[1,128]{1,0:T(1,128)S(1)} %copy-done.4, f32[1,128,128]{2,1,0:T(8,128)S(1)} %copy-done.2), custom_call_target="tpu_custom_call" | custom-call | tf_op jit(solution)/shard_map/own_inverse/pallas_call | solution.py:251
  9.0 0.8 broadcast_in_dim.14
  9.9 5.9 %all-to-all-start = ((f32[8,136,128]{2,1,0:T(8,128)}), f32[8,136,128]{2,1,0:T(8,128)S(1)}, u32[]{:S(2)}, u32[]{:S(2)}) async-start(f32[8,136,128]{2,1,0:T(8,128)} %broadcast_in_dim.14), calls=%async_computation | async-start | bytes 1114112 | tf_op jit(solution)/shard_map/all_to_all | solution.py:273
  15.8 0.0 copy-done.1
  15.8 0.0 copy-done
  15.8 0.7 prepare.1
  16.6 0.9 pad_maximum_fusion
  17.4 5.6 %all-to-all-done.blocks_ref = f32[8,136,128]{2,1,0:T(8,128)S(1)} async-done(((f32[8,136,128]{2,1,0:T(8,128)}), f32[8,136,128]{2,1,0:T(8,128)S(1)}, u32[]{:S(2)}, u32[]{:S(2)}) %all-to-all-start) | async-done | bytes 557088 | tf_op jit(solution)/shard_map/all_to_all | solution.py:273
  23.1 3.7 %all-to-all-start.1 = ((f32[8,160,128]{2,1,0:T(8,128)}), f32[8,160,128]{2,1,0:T(8,128)S(1)}, u32[]{:S(2)}, u32[]{:S(2)}) async-start(f32[8,160,128]{2,1,0:T(8,128)} %pad_maximum_fusion), calls=%async_computation.1 | async-start | bytes 1310720 | tf_op jit(solution)/shard_map/all_to_all | solution.py:271
  26.8 0.0 copy-start.6
  26.8 0.0 copy-start.7
  26.9 7.4 %all-to-all-done.1.first_ref = f32[8,160,128]{2,1,0:T(8,128)S(1)} async-done(((f32[8,160,128]{2,1,0:T(8,128)}), f32[8,160,128]{2,1,0:T(8,128)S(1)}, u32[]{:S(2)}, u32[]{:S(2)}) %all-to-all-start.1) | async-done | bytes 655392 | tf_op jit(solution)/shard_map/all_to_all | solution.py:271
  34.2 18.2 %half.1 = (f32[168,128]{1,0:T(8,128)S(1)}, f32[11,128,256]{2,1,0:T(8,128)S(1)}, f32[8,16,256]{2,1,0:T(8,128)S(1)}) custom-call(s32[2]{0:T(128)S(1)} %pad_add_fusion.side_ref, f32[8,136,128]{2,1,0:T(8,128)S(1)} %all-to-all-done.blocks_ref, f32[8,160,128]{2,1,0:T(8,128)S(1)} %all-to-all-done.1.first_ref), custom_call_target="tpu_custom_call" | custom-call | tf_op jit(solution)/shard_map/half/pallas_call | solution.py:251
  52.4 7.7 %collective-permute-start = (f32[168,128]{1,0:T(8,128)S(1)}, f32[168,128]{1,0:T(8,128)S(1)}, u32[]{:S(2)}, u32[]{:S(2)}) collective-permute-start(f32[168,128]{1,0:T(8,128)S(1)} %get-tuple-element.9.mine_ref), channel_id=1, source_target_pairs={{0,12},{1,13},{2,14},{3,15},{4,8},{5,9},{6,10},{7,11},{8,4},{9,5},... | collective-permute-start | bytes 258056 | tf_op jit(solution)/shard_map/ppermute | solution.py:283
  60.2 1.9 %collective-permute-start.1 = (f32[128,128]{1,0:T(8,128)S(1)}, f32[128,128]{1,0:T(8,128)S(1)}, u32[]{:S(2)}, u32[]{:S(2)}) collective-permute-start(f32[128,128]{1,0:T(8,128)S(1)} %slice_bitcast_fusion.own_link_ref), channel_id=1, source_target_pairs={{0,12},{1,13},{2,14},{3,15},{4,8},{5,9},{6,10},{7,11},{8,4},{9,5},... | collective-permute-start | bytes 196616 | tf_op jit(solution)/shard_map/ppermute | solution.py:282
  62.1 4.6 %collective-permute-done.1.sent_link_ref = f32[128,128]{1,0:T(8,128)S(1)} collective-permute-done((f32[128,128]{1,0:T(8,128)S(1)}, f32[128,128]{1,0:T(8,128)S(1)}, u32[]{:S(2)}, u32[]{:S(2)}) %collective-permute-start.1) | collective-permute-done | bytes 65568 | tf_op jit(solution)/shard_map/ppermute | solution.py:282
  66.7 0.0 collective-permute-done.other_ref
  66.7 14.7 %middle.1 = f32[8,128]{1,0:T(8,128)} custom-call(s32[2]{0:T(128)S(1)} %pad_add_fusion.side_ref, f32[168,128]{1,0:T(8,128)S(1)} %get-tuple-element.9.mine_ref, f32[168,128]{1,0:T(8,128)S(1)} %collective-permute-done.other_ref, f32[128,128]{1,0:T(8,128)S(1)} %slice_bitcast_fusion.own_link_ref, f32[128,128]{1,0:T(8,128)S(1)} %collective-permute-done.1.sent_link_ref, ...), custom_call_target="tpu_custom_call" | custom-call | tf_op jit(solution)/shard_map/middle/pallas_call | solution.py:251
  81.4 3.3 %all-to-all-start.2 = ((f32[8,1,128]{2,1,0:T(1,128)}), f32[8,1,128]{2,1,0:T(1,128)S(1)}, u32[]{:S(2)}, u32[]{:S(2)}) async-start(f32[8,1,128]{2,1,0:T(1,128)} %bitcast.4), calls=%async_computation.2 | async-start | bytes 8192 | tf_op jit(solution)/shard_map/all_to_all | solution.py:285
  84.7 4.8 %all-to-all-done.2 = f32[8,1,128]{2,1,0:T(1,128)S(1)} async-done(((f32[8,1,128]{2,1,0:T(1,128)}), f32[8,1,128]{2,1,0:T(1,128)S(1)}, u32[]{:S(2)}, u32[]{:S(2)}) %all-to-all-start.2) | async-done | bytes 4128 | tf_op jit(solution)/shard_map/all_to_all | solution.py:285
  89.5 0.0 copy-start.5
  89.5 6.2 %all-gather.2 = f32[2,1,128]{2,1,0:T(1,128)S(1)} all-gather(f32[1,1,128]{2,1,0:T(1,128)S(1)} %bitcast.17), channel_id=2, replica_groups={{0,16},{32,48},{64,80},{96,112},{128,144},{160,176},{192,208},{224,240}..., dimensions={0}, use_global_device_ids=true | all-gather | bytes 1536 | tf_op jit(solution)/shard_map/all_gather | solution.py:299
  95.7 3.5 %collective-permute-start.2 = (f32[2,128]{1,0:T(2,128)S(1)}, f32[2,128]{1,0:T(2,128)S(1)}, u32[]{:S(2)}, u32[]{:S(2)}) collective-permute-start(f32[2,128]{1,0:T(2,128)S(1)} %bitcast.13), channel_id=1, source_target_pairs={{16,48},{32,0},{48,80},{64,32},{80,112},{96,64},{112,144},{128,96}... | collective-permute-start | bytes 3080 | tf_op jit(solution)/shard_map/ppermute | solution.py:297
  99.3 0.0 copy-done.6
  99.3 0.0 copy-done.7
  99.3 0.1 fusion
  99.4 0.6 collective-permute-done.2
  100.0 4.9 %collective-permute-start.3 = (f32[4,128]{1,0:T(4,128)S(1)}, f32[4,128]{1,0:T(4,128)S(1)}, u32[]{:S(2)}, u32[]{:S(2)}) collective-permute-start(f32[4,128]{1,0:T(4,128)S(1)} %pad_maximum_fusion.2), channel_id=1, source_target_pairs={{16,80},{48,112},{64,0},{80,144},{96,32},{112,176},{128,64},{144,2... | collective-permute-start | bytes 6152 | tf_op jit(solution)/shard_map/ppermute | solution.py:297
  105.0 0.7 collective-permute-done.3
  105.7 7.3 %collective-permute-start.4 = (f32[4,128]{1,0:T(4,128)S(1)}, f32[4,128]{1,0:T(4,128)S(1)}, u32[]{:S(2)}, u32[]{:S(2)}) collective-permute-start(f32[4,128]{1,0:T(4,128)S(1)} %collective-permute-done.3), channel_id=1, source_target_pairs={{16,80},{48,112},{64,0},{80,144},{96,32},{112,176},{128,64},{144,2... | collective-permute-start | bytes 6152 | tf_op jit(solution)/shard_map/ppermute | solution.py:297
  113.0 0.1 copy.12
  113.1 0.6 collective-permute-done.4
  113.7 0.1 multiply_reduce_fusion
  113.8 3.9 %all-gather.3 = f32[2,2,128]{2,1,0:T(2,128)S(1)} all-gather(f32[1,2,128]{2,1,0:T(2,128)S(1)} %bitcast.16), channel_id=3, replica_groups={{0,16},{32,48},{64,80},{96,112},{128,144},{160,176},{192,208},{224,240}..., dimensions={0}, use_global_device_ids=true | all-gather | bytes 3072 | tf_op jit(solution)/shard_map/all_gather | solution.py:313
  117.7 0.5 dynamic-slice_bitcast_fusion
  118.3 0.0 copy-done.5
  (10 shorter events, 0.1 us)
Async XLA Ops:
  0.6 15.2 %copy-start.1 = (f32[1,128,128]{2,1,0:T(8,128)S(1)}, f32[1,128,128]{2,1,0:T(8,128)}, u32[]{:S(2)}) copy-start(f32[1,128,128]{2,1,0:T(8,128)} %coupling_ref.1) | copy-start | bytes 196612
  0.6 15.2 %copy-start = (f32[2,1,1,128,128]{4,3,2,1,0:T(8,128)S(1)}, f32[2,1,1,128,128]{4,3,2,1,0:T(8,128)}, u32[]{:S(2)}) copy-start(f32[2,1,1,128,128]{4,3,2,1,0:T(8,128)} %source_ref.1) | copy-start | bytes 393220
  1.4 0.8 copy-start.2
  2.3 0.7 copy-start.3
  2.9 0.7 copy-start.4
  9.9 13.2 %all-to-all-start = ((f32[8,136,128]{2,1,0:T(8,128)}), f32[8,136,128]{2,1,0:T(8,128)S(1)}, u32[]{:S(2)}, u32[]{:S(2)}) async-start(f32[8,136,128]{2,1,0:T(8,128)} %broadcast_in_dim.14), calls=%async_computation | async-start | bytes 1114112 | tf_op jit(solution)/shard_map/all_to_all | solution.py:273
  23.1 11.1 %all-to-all-start.1 = ((f32[8,160,128]{2,1,0:T(8,128)}), f32[8,160,128]{2,1,0:T(8,128)S(1)}, u32[]{:S(2)}, u32[]{:S(2)}) async-start(f32[8,160,128]{2,1,0:T(8,128)} %pad_maximum_fusion), calls=%async_computation.1 | async-start | bytes 1310720 | tf_op jit(solution)/shard_map/all_to_all | solution.py:271
  26.8 72.5 %copy-start.6 = (f32[6]{0:T(128)S(1)}, f32[6]{0:T(128)}, u32[]{:S(2)}) copy-start(f32[6]{0:T(128)} %param.14) | copy-start | bytes 76
  26.8 72.5 %copy-start.7 = (s32[6]{0:T(128)S(1)}, s32[6]{0:T(128)}, u32[]{:S(2)}) copy-start(s32[6]{0:T(128)} %param.15) | copy-start | bytes 76
  52.4 14.3 %collective-permute-start = (f32[168,128]{1,0:T(8,128)S(1)}, f32[168,128]{1,0:T(8,128)S(1)}, u32[]{:S(2)}, u32[]{:S(2)}) collective-permute-start(f32[168,128]{1,0:T(8,128)S(1)} %get-tuple-element.9.mine_ref), channel_id=1, source_target_pairs={{0,12},{1,13},{2,14},{3,15},{4,8},{5,9},{6,10},{7,11},{8,4},{9,5},... | collective-permute-start | bytes 258056 | tf_op jit(solution)/shard_map/ppermute | solution.py:283
  60.2 6.6 %collective-permute-start.1 = (f32[128,128]{1,0:T(8,128)S(1)}, f32[128,128]{1,0:T(8,128)S(1)}, u32[]{:S(2)}, u32[]{:S(2)}) collective-permute-start(f32[128,128]{1,0:T(8,128)S(1)} %slice_bitcast_fusion.own_link_ref), channel_id=1, source_target_pairs={{0,12},{1,13},{2,14},{3,15},{4,8},{5,9},{6,10},{7,11},{8,4},{9,5},... | collective-permute-start | bytes 196616 | tf_op jit(solution)/shard_map/ppermute | solution.py:282
  81.4 8.1 %all-to-all-start.2 = ((f32[8,1,128]{2,1,0:T(1,128)}), f32[8,1,128]{2,1,0:T(1,128)S(1)}, u32[]{:S(2)}, u32[]{:S(2)}) async-start(f32[8,1,128]{2,1,0:T(1,128)} %bitcast.4), calls=%async_computation.2 | async-start | bytes 8192 | tf_op jit(solution)/shard_map/all_to_all | solution.py:285
  89.5 28.8 %copy-start.5 = (f32[128]{0:T(128)}, f32[128]{0:T(128)S(1)}, u32[]{:S(2)}) copy-start(f32[128]{0:T(128)S(1)} %reduce_sum.27) | copy-start | bytes 1540
  95.7 4.2 %collective-permute-start.2 = (f32[2,128]{1,0:T(2,128)S(1)}, f32[2,128]{1,0:T(2,128)S(1)}, u32[]{:S(2)}, u32[]{:S(2)}) collective-permute-start(f32[2,128]{1,0:T(2,128)S(1)} %bitcast.13), channel_id=1, source_target_pairs={{16,48},{32,0},{48,80},{64,32},{80,112},{96,64},{112,144},{128,96}... | collective-permute-start | bytes 3080 | tf_op jit(solution)/shard_map/ppermute | solution.py:297
  100.0 5.7 %collective-permute-start.3 = (f32[4,128]{1,0:T(4,128)S(1)}, f32[4,128]{1,0:T(4,128)S(1)}, u32[]{:S(2)}, u32[]{:S(2)}) collective-permute-start(f32[4,128]{1,0:T(4,128)S(1)} %pad_maximum_fusion.2), channel_id=1, source_target_pairs={{16,80},{48,112},{64,0},{80,144},{96,32},{112,176},{128,64},{144,2... | collective-permute-start | bytes 6152 | tf_op jit(solution)/shard_map/ppermute | solution.py:297
  105.7 8.0 %collective-permute-start.4 = (f32[4,128]{1,0:T(4,128)S(1)}, f32[4,128]{1,0:T(4,128)S(1)}, u32[]{:S(2)}, u32[]{:S(2)}) collective-permute-start(f32[4,128]{1,0:T(4,128)S(1)} %collective-permute-done.3), channel_id=1, source_target_pairs={{16,80},{48,112},{64,0},{80,144},{96,32},{112,176},{128,64},{144,2... | collective-permute-start | bytes 6152 | tf_op jit(solution)/shard_map/ppermute | solution.py:297

commit v2 on v1

--- a/solution.py
+++ b/solution.py
@@ -133,37 +133,48 @@
     return pack(re, im)
 
 
-def prepare_kernel(side_ref, coupling_ref, source_ref, coupling_out, source_out):
-    link = coupling_ref[0]
-    coupling_out[...] = jnp.where(side_ref[0] == 1, link.T, link)
-    for part in range(2):
-        flipped = source_ref[part, 0, 0].T
-        for q in range(HALF):
-            source_out[q, COLS * part : COLS * (part + 1)] = flipped[COLS * q : COLS * (q + 1)]
-
-
-def own_kernel(side_ref, energy_ref, shift_ref, width_ref, onsite_ref, out_ref):
+def sides():
+    place = lax.axis_index("transpor")
+    right = (place >= HALF).astype(jnp.int32)
+    return right, jnp.bitwise_xor(lax.rem(place, 2), right) == 0
+
+
+def own_kernel(*refs):
+    inputs, out_ref, held, arrived = refs[:6], refs[6], refs[7:13], refs[13]
+    copies = [pltpu.make_async_copy(a, b, arrived.at[k]) for k, (a, b) in enumerate(zip(inputs, held))]
+    for copy in copies:
+        copy.start()
+    for copy in copies:
+        copy.wait()
+    energy_ref, shift_ref, width_ref, onsite_ref, coupling_ref, source_ref = held
+    right, first = sides()
     i, j = iota((N, N), 0), iota((N, N), 1)
-    re = jnp.where(i == j, energy_ref[0] - shift_ref[...], 0.0) - onsite_ref[0]
+    re = jnp.where(i == j, energy_ref[...] - shift_ref[...], 0.0) - onsite_ref[0]
     im = jnp.where(i == j, broadening + width_ref[...], 0.0)
     block = pack(re, im)
-
-    @pl.when(side_ref[1] == 0)
-    def _():
-        out_ref[...] = fold(invert([block])[0])
-
-    @pl.when(side_ref[1] == 1)
-    def _():
-        out_ref[...] = fold(block)
-
-
-def half_kernel(side_ref, blocks_ref, first_ref, mid_ref, w_ref, y_ref):
-    right = side_ref[0]
+    link = coupling_ref[0]
+    link = jnp.where(right == 1, link.T, link)
+    flipped = [source_ref[part, 0, 0].T for part in range(2)]
+    for q in range(HALF):
+        out_ref[q, PACK : PACK + N] = link
+        for part in range(2):
+            row = PACK + N + COLS * part
+            out_ref[q, row : row + COLS] = flipped[part][COLS * q : COLS * (q + 1)]
+    value = fold(jnp.where(first, invert([block])[0], block))
+    for q in range(HALF):
+        out_ref[q, :PACK] = value
+
+
+def half_kernel(got_ref, mid_ref, w_ref, y_ref):
+    right, _ = sides()
     place = [jnp.bitwise_xor(m, 3 * right) for m in range(HALF)]
     link_place = [jnp.where(right == 1, place[m], m + 1) for m in range(HALF - 1)]
-    U = [first_ref[link_place[m], :N] for m in range(HALF - 1)]
-    blocks = [unfold(blocks_ref[place[m]]) for m in range(HALF)]
-    z = [pack(first_ref[place[m], N : N + COLS], first_ref[place[m], N + COLS :]) for m in range(HALF)]
+    U = [got_ref[link_place[m], PACK : PACK + N] for m in range(HALF - 1)]
+    blocks = [unfold(got_ref[place[m], :PACK]) for m in range(HALF)]
+    z = [
+        pack(got_ref[place[m], PACK + N : PACK + N + COLS], got_ref[place[m], PACK + N + COLS :])
+        for m in range(HALF)
+    ]
     D = {m: blocks[m] for m in range(1, HALF, 2)}
     UT = [u.T for u in U]
     V = {}
@@ -215,17 +226,18 @@
     z[7] = z[7] + times(z[3], w3r)
     mid_ref[:PACK] = fold(D[7])
     mid_ref[PACK : PACK + COLS] = z[7][:, :N]
-    mid_ref[PACK + COLS :] = z[7][:, N:]
-
-
-def middle_kernel(side_ref, mine_ref, other_ref, own_link_ref, sent_link_ref, w_ref, y_ref, out_ref):
-    right = side_ref[0]
-    sent = sent_link_ref[...]
-    U = jnp.where(right == 1, own_link_ref[...], sent.T)
-    UT = jnp.where(right == 1, own_link_ref[...].T, sent)
+    mid_ref[PACK + COLS : PACK + 2 * COLS] = z[7][:, N:]
+    mid_ref[PACK + 2 * COLS :] = got_ref[4, PACK : PACK + N]
+
+
+def middle_kernel(mine_ref, other_ref, w_ref, y_ref, out_ref):
+    right, _ = sides()
+    link = jnp.where(right == 1, mine_ref[PACK + 2 * COLS :], other_ref[PACK + 2 * COLS :])
+    U = jnp.where(right == 1, link, link.T)
+    UT = jnp.where(right == 1, link.T, link)
     mine = unfold(mine_ref[:PACK])
-    z = pack(mine_ref[PACK : PACK + COLS], mine_ref[PACK + COLS :])
-    z_other = pack(other_ref[PACK : PACK + COLS], other_ref[PACK + COLS :])
+    z = pack(mine_ref[PACK : PACK + COLS], mine_ref[PACK + COLS : PACK + 2 * COLS])
+    z_other = pack(other_ref[PACK : PACK + COLS], other_ref[PACK + COLS : PACK + 2 * COLS])
     (q,) = invert([unfold(other_ref[:PACK])])
     w = dot(jnp.concatenate([q[:, :N], q[:, N:]], axis=0), UT)
     w = pack(w[:N], w[N:])
@@ -244,44 +256,37 @@
         out_ref[jnp.bitwise_xor(m, 3 * right)] = total[0]
 
 
-def call(kernel, shapes, smem, operands, name):
+def call(kernel, shapes, operands, name, streamed=False):
     vmem = pl.BlockSpec(memory_space=pltpu.VMEM)
-    scalar = pl.BlockSpec(memory_space=pltpu.SMEM)
     many = isinstance(shapes, list)
+    extra = {}
+    inputs = [vmem] * len(operands)
+    if streamed:
+        inputs = [pl.BlockSpec(memory_space=pltpu.HBM)] * len(operands)
+        held = [pltpu.VMEM(v.shape, f32) for v in operands]
+        extra = dict(scratch_shapes=held + [pltpu.SemaphoreType.DMA((len(operands),))])
     return pl.pallas_call(
         kernel,
         out_shape=[jax.ShapeDtypeStruct(s, f32) for s in shapes] if many else jax.ShapeDtypeStruct(shapes, f32),
-        in_specs=[scalar] * smem + [vmem] * (len(operands) - smem),
+        in_specs=inputs,
         out_specs=[vmem] * len(shapes) if many else vmem,
-        compiler_params=pltpu.CompilerParams(vmem_limit_bytes=40 * 2**20),
+        compiler_params=pltpu.CompilerParams(vmem_limit_bytes=(60 if streamed else 40) * 2**20),
         name=name,
+        **extra,
     )(*operands)
 
 
 def on_device(energy_level, sigma_real, sigma_width, onsite, coupling, source, mode_strength, mode_shift):
-    place = lax.axis_index("transpor")
-    right = (place >= HALF).astype(jnp.int32)
-    odd = jnp.bitwise_xor(place % 2, right)
-    side = jnp.stack([right, odd])
     exchange = functools.partial(
         lax.all_to_all, axis_name="transpor", split_axis=0, concat_axis=0, axis_index_groups=GROUPS, tiled=True
     )
-
-    link, columns = call(prepare_kernel, [(N, N), (HALF, 2 * COLS, N)], 1, (side, coupling, source), "prepare")
-    first = exchange(jnp.concatenate([jnp.broadcast_to(link, (HALF, N, N)), columns], axis=1))
-    own = call(own_kernel, (PACK, N), 2, (side, energy_level, sigma_real, sigma_width, onsite), "own_inverse")
-    blocks = exchange(jnp.broadcast_to(own, (HALF, PACK, N)))
+    operands = (energy_level.reshape(1, 1), sigma_real, sigma_width, onsite, coupling, source)
+    got = exchange(call(own_kernel, (HALF, PACK + N + 2 * COLS, N), operands, "own_inverse", True))
     middle, w, y = call(
-        half_kernel,
-        [(PACK + 2 * COLS, N), (11, N, 2 * N), (HALF, COLS, 2 * N)],
-        1,
-        (side, blocks, first),
-        "half",
+        half_kernel, [(PACK + 2 * COLS + N, N), (11, N, 2 * N), (HALF, COLS, 2 * N)], (got,), "half"
     )
-    own_link = first[4, :N]
-    sent_link = lax.ppermute(own_link, "transpor", MIRROR)
     other = lax.ppermute(middle, "transpor", MIRROR)
-    sums = call(middle_kernel, (HALF, N), 1, (side, middle, other, own_link, sent_link, w, y), "middle")
+    sums = call(middle_kernel, (HALF, N), (middle, other, w, y), "middle")
     density = jnp.sum(exchange(sums), axis=0, keepdims=True)
     return (density, mix(density, mode_strength, mode_shift))
 

time: 120 us -> 108 us (0.900)
  blocking collectives: 10.2 us -> 29.1 us
  waiting for transfers between devices: 24.3 us -> 9.36 us
  starting transfers between devices: 38.4 us -> 26.8 us
  local copies, waits for them, and re-layouts: 3.67 us -> 0.63 us
    all_to_all x0 -> x1, blocking collectives: none -> 18.3 us  [on_device(): exchange(call(own_kernel, (HALF, PACK + N + 2 * COLS, N), operands, 'own_...]
    all_to_all x2 -> x0, waiting for transfers between devices: 13 us -> none  [the longest x1 7.37 us: on_device(): exchange(jnp.concatenate([jnp.broadcast_to(link, (HALF, N, N)), columns],...]
    all_to_all x2 -> x0, starting transfers between devices: 9.67 us -> none  [the longest x1 5.95 us: on_device(): blocks = exchange(jnp.broadcast_to(own, (HALF, PACK, N)))]
    ppermute x1 -> x0, waiting for transfers between devices: 4.62 us -> none  [on_device(): sent_link = lax.ppermute(own_link, 'transpor', MIRROR)]
    ppermute x1, waiting for transfers between devices: 0.01 us -> 2.53 us  [on_device(): other = lax.ppermute(middle, 'transpor', MIRROR)]
    unnamed x16 -> x6, local copies, waits for them, and re-layouts: 2.17 us -> 0.02 us
    ppermute x1 -> x0, starting transfers between devices: 1.92 us -> none  [on_device(): sent_link = lax.ppermute(own_link, 'transpor', MIRROR)]
    pallas_call x4 -> x3, Pallas kernels: 39 us -> 38.8 us  [call(): pl.pallas_call(kernel, out_shape=[jax.ShapeDtypeStruct(s, f32) for s in s...]
  transfers between devices with their start and end apart: 8 -> 5, of which waited for: 7 -> 5; matrix products, arithmetic and copies ran while one was open for 1% -> 0% of each run, Pallas kernels for 1% -> 0%
where the time goes in v2:
time: 108 us; the launch traced here: 106 us
  Pallas kernels  38.8 us (36%)
  blocking collectives  29.1 us (27%)
  starting transfers between devices  26.8 us (25%)
  waiting for transfers between devices  9.36 us (9%)
  between operations  1.42 us (1%)
    pallas_call x3, Pallas kernels, call(): pl.pallas_call(kernel, out_shape=[jax.ShapeDtypeStruct(s, f32) for s in s...  38.8 us
    all_to_all x1, blocking collectives, on_device(): exchange(call(own_kernel, (HALF, PACK + N + 2 * COLS, N), operands, 'own_...  18.3 us
    ppermute x3, starting transfers between devices, fetch(): lax.ppermute(value, 'energy', [(a, b) for a, b in steps if 0 <= b < energ...  15.9 us
    ppermute x1, starting transfers between devices, on_device(): other = lax.ppermute(middle, 'transpor', MIRROR)  7.57 us
    all_gather x1, blocking collectives, mix(): lax.all_gather(density, 'energy', axis_index_groups=couples, tiled=True)  6.79 us
    all_to_all x1, waiting for transfers between devices, on_device(): density = jnp.sum(exchange(sums), axis=0, keepdims=True)  4.92 us
    all_gather x1, blocking collectives, mix(): both = lax.all_gather(partial, 'energy', axis_index_groups=couples)  3.94 us
    all_to_all x1, starting transfers between devices, on_device(): density = jnp.sum(exchange(sums), axis=0, keepdims=True)  3.28 us
  transfers between devices with their start and end apart: 5, of which 5 were waited for; matrix products, arithmetic and copies ran while one was open for 0% of the time, Pallas kernels for 0%

profile of v2, /device:TPU:1, one launch (start us, length us, event | category | flops | bytes accessed | tf_op | source)
XLA Modules:
  0.0 106.3 jit_solution(8650411019622853994)
XLA Ops:
  1.3 7.0 %own_inverse.1 = f32[8,296,128]{2,1,0:T(8,128)} custom-call(f32[1,1]{1,0:T(1,128)} %bitcast.10.refs_0_, f32[1,128]{1,0:T(1,128)} %refs_1_.1, f32[1,128]{1,0:T(1,128)} %refs_2_.1, f32[1,128,128]{2,1,0:T(8,128)} %refs_3_.1, f32[1,128,128]{2,1,0:T(8,128)} %refs_4_.1, f32[2,1,1,128,128]{4,3,2,1,0:T(8,128)} %refs_5_.1), custom_call_target="tpu_custom_call" | custom-call | tf_op jit(solution)/shard_map/own_inverse/pallas_call | solution.py:268
  8.3 18.3 %all_to_all.14.got_ref = f32[8,296,128]{2,1,0:T(8,128)S(1)} all-to-all(f32[8,296,128]{2,1,0:T(8,128)} %own_inverse.1), channel_id=1, replica_groups={{0,1,2,3,4,5,6,7},{12,13,14,15,8,9,10,11},{16,17,18,19,20,21,22,23},{28..., dimensions={0} | all-to-all | bytes 2424832 | tf_op jit(solution)/shard_map/all_to_all | solution.py:284
  26.7 17.7 %half.1 = (f32[296,128]{1,0:T(8,128)S(1)}, f32[11,128,256]{2,1,0:T(8,128)S(1)}, f32[8,16,256]{2,1,0:T(8,128)S(1)}) custom-call(f32[8,296,128]{2,1,0:T(8,128)S(1)} %all_to_all.14.got_ref), custom_call_target="tpu_custom_call" | custom-call | tf_op jit(solution)/shard_map/half/pallas_call | solution.py:268
  44.3 0.0 copy-start.1
  44.3 0.0 copy-start.2
  44.4 7.6 %collective-permute-start = (f32[296,128]{1,0:T(8,128)S(1)}, f32[296,128]{1,0:T(8,128)S(1)}, u32[]{:S(2)}, u32[]{:S(2)}) collective-permute-start(f32[296,128]{1,0:T(8,128)S(1)} %get-tuple-element.5.mine_ref), channel_id=1, source_target_pairs={{0,12},{1,13},{2,14},{3,15},{4,8},{5,9},{6,10},{7,11},{8,4},{9,5},... | collective-permute-start | bytes 454664 | tf_op jit(solution)/shard_map/ppermute | solution.py:288
  52.0 2.5 %collective-permute-done.other_ref = f32[296,128]{1,0:T(8,128)S(1)} collective-permute-done((f32[296,128]{1,0:T(8,128)S(1)}, f32[296,128]{1,0:T(8,128)S(1)}, u32[]{:S(2)}, u32[]{:S(2)}) %collective-permute-start) | collective-permute-done | bytes 151584 | tf_op jit(solution)/shard_map/ppermute | solution.py:288
  54.5 14.1 %middle.1 = f32[8,128]{1,0:T(8,128)} custom-call(f32[296,128]{1,0:T(8,128)S(1)} %get-tuple-element.5.mine_ref, f32[296,128]{1,0:T(8,128)S(1)} %collective-permute-done.other_ref, f32[11,128,256]{2,1,0:T(8,128)S(1)} %get-tuple-element.6.w_ref, f32[8,16,256]{2,1,0:T(8,128)S(1)} %get-tuple-element.7.y_ref), custom_call_target="tpu_custom_call" | custom-call | tf_op jit(solution)/shard_map/middle/pallas_call | solution.py:268
  68.6 3.3 %all-to-all-start.1 = ((f32[8,1,128]{2,1,0:T(1,128)}), f32[8,1,128]{2,1,0:T(1,128)S(1)}, u32[]{:S(2)}, u32[]{:S(2)}) async-start(f32[8,1,128]{2,1,0:T(1,128)} %bitcast.2), calls=%async_computation.1 | async-start | bytes 8192 | tf_op jit(solution)/shard_map/all_to_all | solution.py:290
  71.9 4.9 %all-to-all-done.1 = f32[8,1,128]{2,1,0:T(1,128)S(1)} async-done(((f32[8,1,128]{2,1,0:T(1,128)}), f32[8,1,128]{2,1,0:T(1,128)S(1)}, u32[]{:S(2)}, u32[]{:S(2)}) %all-to-all-start.1) | async-done | bytes 4128 | tf_op jit(solution)/shard_map/all_to_all | solution.py:290
  76.9 0.0 copy-start
  76.9 6.8 %all-gather.2 = f32[2,1,128]{2,1,0:T(1,128)S(1)} all-gather(f32[1,1,128]{2,1,0:T(1,128)S(1)} %bitcast.15), channel_id=2, replica_groups={{0,16},{32,48},{64,80},{96,112},{128,144},{160,176},{192,208},{224,240}..., dimensions={0}, use_global_device_ids=true | all-gather | bytes 1536 | tf_op jit(solution)/shard_map/all_gather | solution.py:304
  83.6 3.7 %collective-permute-start.1 = (f32[2,128]{1,0:T(2,128)S(1)}, f32[2,128]{1,0:T(2,128)S(1)}, u32[]{:S(2)}, u32[]{:S(2)}) collective-permute-start(f32[2,128]{1,0:T(2,128)S(1)} %bitcast.11), channel_id=1, source_target_pairs={{16,48},{32,0},{48,80},{64,32},{80,112},{96,64},{112,144},{128,96}... | collective-permute-start | bytes 3080 | tf_op jit(solution)/shard_map/ppermute | solution.py:302
  87.3 0.0 copy-done.1
  87.3 0.0 copy-done.2
  87.3 0.1 fusion
  87.4 0.6 collective-permute-done.1
  88.0 4.9 %collective-permute-start.2 = (f32[4,128]{1,0:T(4,128)S(1)}, f32[4,128]{1,0:T(4,128)S(1)}, u32[]{:S(2)}, u32[]{:S(2)}) collective-permute-start(f32[4,128]{1,0:T(4,128)S(1)} %pad_maximum_fusion.1), channel_id=1, source_target_pairs={{16,80},{48,112},{64,0},{80,144},{96,32},{112,176},{128,64},{144,2... | collective-permute-start | bytes 6152 | tf_op jit(solution)/shard_map/ppermute | solution.py:302
  93.0 0.7 collective-permute-done.2
  93.7 7.3 %collective-permute-start.3 = (f32[4,128]{1,0:T(4,128)S(1)}, f32[4,128]{1,0:T(4,128)S(1)}, u32[]{:S(2)}, u32[]{:S(2)}) collective-permute-start(f32[4,128]{1,0:T(4,128)S(1)} %collective-permute-done.2), channel_id=1, source_target_pairs={{16,80},{48,112},{64,0},{80,144},{96,32},{112,176},{128,64},{144,2... | collective-permute-start | bytes 6152 | tf_op jit(solution)/shard_map/ppermute | solution.py:302
  101.0 0.1 copy.12
  101.1 0.6 collective-permute-done.3
  101.7 0.1 multiply_reduce_fusion
  101.8 3.9 %all-gather.3 = f32[2,2,128]{2,1,0:T(2,128)S(1)} all-gather(f32[1,2,128]{2,1,0:T(2,128)S(1)} %bitcast.14), channel_id=3, replica_groups={{0,16},{32,48},{64,80},{96,112},{128,144},{160,176},{192,208},{224,240}..., dimensions={0}, use_global_device_ids=true | all-gather | bytes 3072 | tf_op jit(solution)/shard_map/all_gather | solution.py:318
  105.8 0.5 dynamic-slice_bitcast_fusion
  106.3 0.0 copy-done
  (8 shorter events, 0.1 us)
Async XLA Ops:
  44.3 43.0 %copy-start.1 = (f32[6]{0:T(128)S(1)}, f32[6]{0:T(128)}, u32[]{:S(2)}) copy-start(f32[6]{0:T(128)} %param.14) | copy-start | bytes 76
  44.3 43.0 %copy-start.2 = (s32[6]{0:T(128)S(1)}, s32[6]{0:T(128)}, u32[]{:S(2)}) copy-start(s32[6]{0:T(128)} %param.15) | copy-start | bytes 76
  44.4 10.1 %collective-permute-start = (f32[296,128]{1,0:T(8,128)S(1)}, f32[296,128]{1,0:T(8,128)S(1)}, u32[]{:S(2)}, u32[]{:S(2)}) collective-permute-start(f32[296,128]{1,0:T(8,128)S(1)} %get-tuple-element.5.mine_ref), channel_id=1, source_target_pairs={{0,12},{1,13},{2,14},{3,15},{4,8},{5,9},{6,10},{7,11},{8,4},{9,5},... | collective-permute-start | bytes 454664 | tf_op jit(solution)/shard_map/ppermute | solution.py:288
  68.6 8.2 %all-to-all-start.1 = ((f32[8,1,128]{2,1,0:T(1,128)}), f32[8,1,128]{2,1,0:T(1,128)S(1)}, u32[]{:S(2)}, u32[]{:S(2)}) async-start(f32[8,1,128]{2,1,0:T(1,128)} %bitcast.2), calls=%async_computation.1 | async-start | bytes 8192 | tf_op jit(solution)/shard_map/all_to_all | solution.py:290
  76.9 29.4 %copy-start = (f32[128]{0:T(128)}, f32[128]{0:T(128)S(1)}, u32[]{:S(2)}) copy-start(f32[128]{0:T(128)S(1)} %reduce_sum.27) | copy-start | bytes 1540
  83.6 4.4 %collective-permute-start.1 = (f32[2,128]{1,0:T(2,128)S(1)}, f32[2,128]{1,0:T(2,128)S(1)}, u32[]{:S(2)}, u32[]{:S(2)}) collective-permute-start(f32[2,128]{1,0:T(2,128)S(1)} %bitcast.11), channel_id=1, source_target_pairs={{16,48},{32,0},{48,80},{64,32},{80,112},{96,64},{112,144},{128,96}... | collective-permute-start | bytes 3080 | tf_op jit(solution)/shard_map/ppermute | solution.py:302
  88.0 5.7 %collective-permute-start.2 = (f32[4,128]{1,0:T(4,128)S(1)}, f32[4,128]{1,0:T(4,128)S(1)}, u32[]{:S(2)}, u32[]{:S(2)}) collective-permute-start(f32[4,128]{1,0:T(4,128)S(1)} %pad_maximum_fusion.1), channel_id=1, source_target_pairs={{16,80},{48,112},{64,0},{80,144},{96,32},{112,176},{128,64},{144,2... | collective-permute-start | bytes 6152 | tf_op jit(solution)/shard_map/ppermute | solution.py:302
  93.7 8.0 %collective-permute-start.3 = (f32[4,128]{1,0:T(4,128)S(1)}, f32[4,128]{1,0:T(4,128)S(1)}, u32[]{:S(2)}, u32[]{:S(2)}) collective-permute-start(f32[4,128]{1,0:T(4,128)S(1)} %collective-permute-done.2), channel_id=1, source_target_pairs={{16,80},{48,112},{64,0},{80,144},{96,32},{112,176},{128,64},{144,2... | collective-permute-start | bytes 6152 | tf_op jit(solution)/shard_map/ppermute | solution.py:302

commit v3 on v2

--- a/solution.py
+++ b/solution.py
@@ -14,6 +14,7 @@
 PACK = N + 8
 broadening = 0.2
 prec = lax.Precision.HIGHEST
+column_prec = lax.Precision.HIGH
 f32 = jnp.float32
 
 GROUPS = [list(range(8)), [12, 13, 14, 15, 8, 9, 10, 11]]
@@ -21,7 +22,8 @@
 
 
 def dot(a, b, dims=((1,), (0,))):
-    return lax.dot_general(a, b, (dims, ((), ())), precision=prec, preferred_element_type=f32)
+    by = column_prec if a.shape[0] == COLS else prec
+    return lax.dot_general(a, b, (dims, ((), ())), precision=by, preferred_element_type=f32)
 
 
 def lanes_of(v, k):
@@ -293,30 +295,12 @@
 
 def mix(density, mode_strength, mode_shift):
     energies = lax.axis_size("energy")
-    index = lax.axis_index("energy")
-    odd = index % 2
-    couples = [[e, e + 1] for e in range(0, energies, 2)]
-
-    def fetch(value, chips):
-        steps = [(e, e - 2 * chips if e % 2 == 0 else e + 2 * chips) for e in range(energies)]
-        return lax.ppermute(value, "energy", [(a, b) for a, b in steps if 0 <= b < energies])
-
-    own = lax.all_gather(density, "energy", axis_index_groups=couples, tiled=True)
-    near = jnp.concatenate([own, fetch(own, 1)], axis=0)
-    middle = fetch(near, 2)
-    far = fetch(middle, 2)
-    window = jnp.concatenate([near, middle, far], axis=0)
-    row = jnp.arange(window.shape[0], dtype=jnp.int32)
-    chip = row // 2
-    offset = jnp.where(odd == 1, -chip, chip) * 2 + row % 2
-    used = jnp.where((odd == 1) & (chip == 0), 0.0, 1.0)
-    target = jnp.arange(2, dtype=jnp.int32)
-    distance = jnp.abs(offset[None, :] - target[:, None])
-    hits = (distance[None] == mode_shift[:, None, None]).astype(f32)
-    weights = jnp.sum(mode_strength[:, None, None] * hits, axis=0) * used
-    partial = jnp.sum(weights[:, :, None] * window[None], axis=1)
-    both = lax.all_gather(partial, "energy", axis_index_groups=couples)
-    return lax.dynamic_slice_in_dim(both[0] + both[1], odd, 1, axis=0)
+    everywhere = jnp.broadcast_to(density, (energies, N))
+    every = lax.all_to_all(everywhere, "energy", 0, 0, tiled=True)
+    distance = jnp.abs(jnp.arange(energies, dtype=jnp.int32) - lax.axis_index("energy"))
+    hits = (distance[None] == mode_shift[:, None]).astype(f32)
+    weights = jnp.sum(mode_strength[:, None] * hits, axis=0)
+    return jnp.sum(weights[:, None] * every, axis=0, keepdims=True)
 
 
 def solution(mesh):

time: 108 us -> 109 us (level); the launches traced: 106 us -> 109 us
  blocking collectives: 29.1 us -> 18.3 us
  waiting for transfers between devices: 9.36 us -> 19.1 us
  starting transfers between devices: 26.8 us -> 31.6 us
  Pallas kernels: 38.8 us -> 37.3 us
    all_to_all x0 -> x1, starting transfers between devices: none -> 20.7 us  [mix(): every = lax.all_to_all(everywhere, 'energy', 0, 0, tiled=True)]
    ppermute x3 -> x0, starting transfers between devices: 15.9 us -> none  [fetch(): lax.ppermute(value, 'energy', [(a, b) for a, b in steps if 0 <= b < energ...]
    all_to_all x0 -> x1, waiting for transfers between devices: none -> 11.7 us  [mix(): every = lax.all_to_all(everywhere, 'energy', 0, 0, tiled=True)]
    all_gather x2 -> x0, blocking collectives: 10.7 us -> none  [the longest x1 6.79 us: mix(): lax.all_gather(density, 'energy', axis_index_groups=couples, tiled=True)]
    ppermute x3 -> x0, waiting for transfers between devices: 1.91 us -> none  [fetch(): lax.ppermute(value, 'energy', [(a, b) for a, b in steps if 0 <= b < energ...]
    pallas_call x3, Pallas kernels: 38.8 us -> 37.3 us  [call(): pl.pallas_call(kernel, out_shape=[jax.ShapeDtypeStruct(s, f32) for s in s...]
  transfers between devices with their start and end apart: 5 -> 3, of which waited for: 5 -> 3; matrix products, arithmetic and copies ran while one was open for 0% -> 0% of each run, Pallas kernels for 0% -> 0%
where the time goes in v3:
time: 109 us
  Pallas kernels  37.3 us (34%)
  starting transfers between devices  31.6 us (29%)
  waiting for transfers between devices  19.1 us (18%)
  blocking collectives  18.3 us (17%)
  between operations  1.35 us (1%)
    pallas_call x3, Pallas kernels, call(): pl.pallas_call(kernel, out_shape=[jax.ShapeDtypeStruct(s, f32) for s in s...  37.3 us
    all_to_all x1, starting transfers between devices, mix(): every = lax.all_to_all(everywhere, 'energy', 0, 0, tiled=True)  20.7 us
    all_to_all x1, blocking collectives, on_device(): exchange(call(own_kernel, (HALF, PACK + N + 2 * COLS, N), operands, 'own_...  18.3 us
    all_to_all x1, waiting for transfers between devices, mix(): every = lax.all_to_all(everywhere, 'energy', 0, 0, tiled=True)  11.7 us
    ppermute x1, starting transfers between devices, on_device(): other = lax.ppermute(middle, 'transpor', MIRROR)  7.72 us
    all_to_all x1, waiting for transfers between devices, on_device(): density = jnp.sum(exchange(sums), axis=0, keepdims=True)  4.92 us
    all_to_all x1, starting transfers between devices, on_device(): density = jnp.sum(exchange(sums), axis=0, keepdims=True)  3.25 us
    ppermute x1, waiting for transfers between devices, on_device(): other = lax.ppermute(middle, 'transpor', MIRROR)  2.56 us
  transfers between devices with their start and end apart: 3, of which 3 were waited for; matrix products, arithmetic and copies ran while one was open for 0% of the time, Pallas kernels for 0%

profile of v3, /device:TPU:1, one launch (start us, length us, event | category | flops | bytes accessed | tf_op | source)
XLA Modules:
  0.0 109.1 jit_solution(7632194504106711469)
XLA Ops:
  1.3 7.0 %own_inverse.1 = f32[8,296,128]{2,1,0:T(8,128)} custom-call(f32[1,1]{1,0:T(1,128)} %bitcast.7.refs_0_, f32[1,128]{1,0:T(1,128)} %refs_1_.1, f32[1,128]{1,0:T(1,128)} %refs_2_.1, f32[1,128,128]{2,1,0:T(8,128)} %refs_3_.1, f32[1,128,128]{2,1,0:T(8,128)} %refs_4_.1, f32[2,1,1,128,128]{4,3,2,1,0:T(8,128)} %refs_5_.1), custom_call_target="tpu_custom_call" | custom-call | tf_op jit(solution)/shard_map/own_inverse/pallas_call | solution.py:270
  8.3 18.3 %all_to_all.23.got_ref = f32[8,296,128]{2,1,0:T(8,128)S(1)} all-to-all(f32[8,296,128]{2,1,0:T(8,128)} %own_inverse.1), channel_id=1, replica_groups={{0,1,2,3,4,5,6,7},{12,13,14,15,8,9,10,11},{16,17,18,19,20,21,22,23},{28..., dimensions={0} | all-to-all | bytes 2424832 | tf_op jit(solution)/shard_map/all_to_all | solution.py:286
  26.7 17.5 %half.1 = (f32[296,128]{1,0:T(8,128)S(1)}, f32[11,128,256]{2,1,0:T(8,128)S(1)}, f32[8,16,256]{2,1,0:T(8,128)S(1)}) custom-call(f32[8,296,128]{2,1,0:T(8,128)S(1)} %all_to_all.23.got_ref), custom_call_target="tpu_custom_call" | custom-call | tf_op jit(solution)/shard_map/half/pallas_call | solution.py:270
  44.2 0.0 copy-start.1
  44.2 0.0 copy-start.2
  44.2 7.7 %collective-permute-start = (f32[296,128]{1,0:T(8,128)S(1)}, f32[296,128]{1,0:T(8,128)S(1)}, u32[]{:S(2)}, u32[]{:S(2)}) collective-permute-start(f32[296,128]{1,0:T(8,128)S(1)} %get-tuple-element.5.mine_ref), channel_id=1, source_target_pairs={{0,12},{1,13},{2,14},{3,15},{4,8},{5,9},{6,10},{7,11},{8,4},{9,5},... | collective-permute-start | bytes 454664 | tf_op jit(solution)/shard_map/ppermute | solution.py:290
  51.9 2.6 %collective-permute-done.other_ref = f32[296,128]{1,0:T(8,128)S(1)} collective-permute-done((f32[296,128]{1,0:T(8,128)S(1)}, f32[296,128]{1,0:T(8,128)S(1)}, u32[]{:S(2)}, u32[]{:S(2)}) %collective-permute-start) | collective-permute-done | bytes 151584 | tf_op jit(solution)/shard_map/ppermute | solution.py:290
  54.5 12.7 %middle.1 = f32[8,128]{1,0:T(8,128)} custom-call(f32[296,128]{1,0:T(8,128)S(1)} %get-tuple-element.5.mine_ref, f32[296,128]{1,0:T(8,128)S(1)} %collective-permute-done.other_ref, f32[11,128,256]{2,1,0:T(8,128)S(1)} %get-tuple-element.6.w_ref, f32[8,16,256]{2,1,0:T(8,128)S(1)} %get-tuple-element.7.y_ref), custom_call_target="tpu_custom_call" | custom-call | tf_op jit(solution)/shard_map/middle/pallas_call | solution.py:270
  67.2 3.2 %all-to-all-start.1 = ((f32[8,1,128]{2,1,0:T(1,128)}), f32[8,1,128]{2,1,0:T(1,128)S(1)}, u32[]{:S(2)}, u32[]{:S(2)}) async-start(f32[8,1,128]{2,1,0:T(1,128)} %bitcast.2), calls=%async_computation.1 | async-start | bytes 8192 | tf_op jit(solution)/shard_map/all_to_all | solution.py:292
  70.5 4.9 %all-to-all-done.1 = f32[8,1,128]{2,1,0:T(1,128)S(1)} async-done(((f32[8,1,128]{2,1,0:T(1,128)}), f32[8,1,128]{2,1,0:T(1,128)S(1)}, u32[]{:S(2)}, u32[]{:S(2)}) %all-to-all-start.1) | async-done | bytes 4128 | tf_op jit(solution)/shard_map/all_to_all | solution.py:292
  75.4 0.0 copy-start
  75.4 0.6 broadcast_in_dim.7
  76.0 20.7 %all-to-all-start.2 = ((f32[32,1,128]{2,1,0:T(1,128)}), f32[32,1,128]{2,1,0:T(1,128)S(1)}, u32[]{:S(2)}, u32[]{:S(2)}) async-start(f32[32,1,128]{2,1,0:T(1,128)} %broadcast_in_dim.7), calls=%async_computation.2 | async-start | bytes 32768 | tf_op jit(solution)/shard_map/all_to_all | solution.py:299
  96.7 0.0 copy-done.1
  96.7 0.0 copy-done.2
  96.7 0.1 select_reduce_fusion
  96.8 11.7 %all-to-all-done.2 = f32[32,1,128]{2,1,0:T(1,128)S(1)} async-done(((f32[32,1,128]{2,1,0:T(1,128)}), f32[32,1,128]{2,1,0:T(1,128)S(1)}, u32[]{:S(2)}, u32[]{:S(2)}) %all-to-all-start.2) | async-done | bytes 16416 | tf_op jit(solution)/shard_map/all_to_all | solution.py:299
  108.5 0.6 multiply_reduce_fusion
  109.1 0.0 copy-done
  (2 shorter events, 0.0 us)
Async XLA Ops:
  44.2 52.5 %copy-start.1 = (f32[6]{0:T(128)S(1)}, f32[6]{0:T(128)}, u32[]{:S(2)}) copy-start(f32[6]{0:T(128)} %param.14) | copy-start | bytes 76
  44.2 52.5 %copy-start.2 = (s32[6]{0:T(128)S(1)}, s32[6]{0:T(128)}, u32[]{:S(2)}) copy-start(s32[6]{0:T(128)} %param.15) | copy-start | bytes 76
  44.2 10.3 %collective-permute-start = (f32[296,128]{1,0:T(8,128)S(1)}, f32[296,128]{1,0:T(8,128)S(1)}, u32[]{:S(2)}, u32[]{:S(2)}) collective-permute-start(f32[296,128]{1,0:T(8,128)S(1)} %get-tuple-element.5.mine_ref), channel_id=1, source_target_pairs={{0,12},{1,13},{2,14},{3,15},{4,8},{5,9},{6,10},{7,11},{8,4},{9,5},... | collective-permute-start | bytes 454664 | tf_op jit(solution)/shard_map/ppermute | solution.py:290
  67.2 8.2 %all-to-all-start.1 = ((f32[8,1,128]{2,1,0:T(1,128)}), f32[8,1,128]{2,1,0:T(1,128)S(1)}, u32[]{:S(2)}, u32[]{:S(2)}) async-start(f32[8,1,128]{2,1,0:T(1,128)} %bitcast.2), calls=%async_computation.1 | async-start | bytes 8192 | tf_op jit(solution)/shard_map/all_to_all | solution.py:292
  75.4 33.7 %copy-start = (f32[128]{0:T(128)}, f32[128]{0:T(128)S(1)}, u32[]{:S(2)}) copy-start(f32[128]{0:T(128)S(1)} %reduce_sum.27) | copy-start | bytes 1540
  76.0 32.5 %all-to-all-start.2 = ((f32[32,1,128]{2,1,0:T(1,128)}), f32[32,1,128]{2,1,0:T(1,128)S(1)}, u32[]{:S(2)}, u32[]{:S(2)}) async-start(f32[32,1,128]{2,1,0:T(1,128)} %broadcast_in_dim.7), calls=%async_computation.2 | async-start | bytes 32768 | tf_op jit(solution)/shard_map/all_to_all | solution.py:299

commit v4 on v2

--- a/solution.py
+++ b/solution.py
@@ -14,6 +14,7 @@
 PACK = N + 8
 broadening = 0.2
 prec = lax.Precision.HIGHEST
+column_prec = lax.Precision.HIGH
 f32 = jnp.float32
 
 GROUPS = [list(range(8)), [12, 13, 14, 15, 8, 9, 10, 11]]
@@ -21,7 +22,8 @@
 
 
 def dot(a, b, dims=((1,), (0,))):
-    return lax.dot_general(a, b, (dims, ((), ())), precision=prec, preferred_element_type=f32)
+    by = column_prec if a.shape[0] == COLS else prec
+    return lax.dot_general(a, b, (dims, ((), ())), precision=by, preferred_element_type=f32)
 
 
 def lanes_of(v, k):
@@ -183,6 +185,7 @@
     def keep(w):
         w_ref[next(slot)] = w
 
+    solved_left, solved_right = {}, {}
     for m in range(0, HALF, 2):
         p = blocks[m]
         stacked = jnp.concatenate([p[:, :N], p[:, N:]], axis=0)
@@ -194,14 +197,17 @@
             w = dot(stacked, pack(UT[m - 1], U[m]))
             wl = pack(w[:N, :N], w[N:, :N])
             wr = pack(w[:N, N:], w[N:, N:])
-            up = dot(U[m - 1], jnp.concatenate([wl, wr], axis=1))
-            D[m - 1] = D[m - 1] - up[:, : 2 * N]
-            V[m - 1] = up[:, 2 * N :]
+            V[m - 1] = dot(U[m - 1], wr)
             z[m - 1] = z[m - 1] + times(z[m], wl)
             keep(wl)
-        D[m + 1] = D[m + 1] - dot(UT[m], wr)
+            solved_left[m - 1] = wl
         z[m + 1] = z[m + 1] + times(z[m], wr)
         keep(wr)
+        solved_right[m + 1] = wr
+    for m in (1, 3, 5):
+        both = jnp.concatenate([solved_right[m], solved_left[m]], axis=0)
+        D[m] = D[m] - dot(pack(UT[m - 1], U[m]), both)
+    D[7] = D[7] - dot(UT[6], solved_right[7])
 
     p1, p5 = invert([D[1], D[5]])
     y_ref[1] = times(z[1], p1)
@@ -302,10 +308,8 @@
         return lax.ppermute(value, "energy", [(a, b) for a, b in steps if 0 <= b < energies])
 
     own = lax.all_gather(density, "energy", axis_index_groups=couples, tiled=True)
-    near = jnp.concatenate([own, fetch(own, 1)], axis=0)
-    middle = fetch(near, 2)
-    far = fetch(middle, 2)
-    window = jnp.concatenate([near, middle, far], axis=0)
+    near = jnp.concatenate([own, fetch(own, 1), fetch(own, 2)], axis=0)
+    window = jnp.concatenate([near, fetch(near, 3)], axis=0)
     row = jnp.arange(window.shape[0], dtype=jnp.int32)
     chip = row // 2
     offset = jnp.where(odd == 1, -chip, chip) * 2 + row % 2

time: 108 us -> 103 us (0.954); the launches traced: 106 us -> 103 us
  blocking collectives: 29.1 us -> 7.38 us
  waiting for transfers between devices: 9.36 us -> 19.9 us
  starting transfers between devices: 26.8 us -> 35.2 us
    all_to_all x1 -> x0, blocking collectives: 18.3 us -> none  [on_device(): exchange(call(own_kernel, (HALF, PACK + N + 2 * COLS, N), operands, 'own_...]
    all_to_all x0 -> x1, waiting for transfers between devices: none -> 11.2 us  [on_device(): exchange(call(own_kernel, (HALF, PACK + N + 2 * COLS, N), operands, 'own_...]
    all_to_all x0 -> x1, starting transfers between devices: none -> 5.96 us  [on_device(): exchange(call(own_kernel, (HALF, PACK + N + 2 * COLS, N), operands, 'own_...]
    all_gather x1, blocking collectives: 6.79 us -> 4.9 us  [mix(): lax.all_gather(density, 'energy', axis_index_groups=couples, tiled=True)]
    ppermute x1, starting transfers between devices: 7.57 us -> 9.22 us  [on_device(): other = lax.ppermute(middle, 'transpor', MIRROR)]
    all_gather x1, blocking collectives: 3.94 us -> 2.48 us  [mix(): both = lax.all_gather(partial, 'energy', axis_index_groups=couples)]
  transfers between devices with their start and end apart: 5 -> 6, of which waited for: 5 -> 5; matrix products, arithmetic and copies ran while one was open for 0% -> 0% of each run, Pallas kernels for 0% -> 0%
where the time goes in v4:
time: 103 us
  Pallas kernels  37.9 us (37%)
  starting transfers between devices  35.2 us (34%)
  waiting for transfers between devices  19.9 us (19%)
  blocking collectives  7.38 us (7%)
  between operations  1.4 us (1%)
    pallas_call x3, Pallas kernels, call(): pl.pallas_call(kernel, out_shape=[jax.ShapeDtypeStruct(s, f32) for s in s...  37.9 us
    ppermute x3, starting transfers between devices, fetch(): lax.ppermute(value, 'energy', [(a, b) for a, b in steps if 0 <= b < energ...  16.2 us
    all_to_all x1, waiting for transfers between devices, on_device(): exchange(call(own_kernel, (HALF, PACK + N + 2 * COLS, N), operands, 'own_...  11.2 us
    ppermute x1, starting transfers between devices, on_device(): other = lax.ppermute(middle, 'transpor', MIRROR)  9.22 us
    all_to_all x1, starting transfers between devices, on_device(): exchange(call(own_kernel, (HALF, PACK + N + 2 * COLS, N), operands, 'own_...  5.96 us
    all_gather x1, blocking collectives, mix(): lax.all_gather(density, 'energy', axis_index_groups=couples, tiled=True)  4.9 us
    all_to_all x1, waiting for transfers between devices, on_device(): density = jnp.sum(exchange(sums), axis=0, keepdims=True)  4.9 us
    all_to_all x1, starting transfers between devices, on_device(): density = jnp.sum(exchange(sums), axis=0, keepdims=True)  3.79 us
  transfers between devices with their start and end apart: 6, of which 5 were waited for; matrix products, arithmetic and copies ran while one was open for 0% of the time, Pallas kernels for 0%

profile of v4, /device:TPU:1, one launch (start us, length us, event | category | flops | bytes accessed | tf_op | source)
XLA Modules:
  0.0 102.6 jit_solution(8519396895186708079)
XLA Ops:
  1.3 7.0 %own_inverse.1 = f32[8,296,128]{2,1,0:T(8,128)} custom-call(f32[1,1]{1,0:T(1,128)} %bitcast.10.refs_0_, f32[1,128]{1,0:T(1,128)} %refs_1_.1, f32[1,128]{1,0:T(1,128)} %refs_2_.1, f32[1,128,128]{2,1,0:T(8,128)} %refs_3_.1, f32[1,128,128]{2,1,0:T(8,128)} %refs_4_.1, f32[2,1,1,128,128]{4,3,2,1,0:T(8,128)} %refs_5_.1), custom_call_target="tpu_custom_call" | custom-call | tf_op jit(solution)/shard_map/own_inverse/pallas_call | solution.py:274
  8.3 6.0 %all-to-all-start = ((f32[8,296,128]{2,1,0:T(8,128)}), f32[8,296,128]{2,1,0:T(8,128)S(1)}, u32[]{:S(2)}, u32[]{:S(2)}) async-start(f32[8,296,128]{2,1,0:T(8,128)} %own_inverse.1), calls=%async_computation | async-start | bytes 2424832 | tf_op jit(solution)/shard_map/all_to_all | solution.py:290
  14.3 11.2 %all-to-all-done.got_ref = f32[8,296,128]{2,1,0:T(8,128)S(1)} async-done(((f32[8,296,128]{2,1,0:T(8,128)}), f32[8,296,128]{2,1,0:T(8,128)S(1)}, u32[]{:S(2)}, u32[]{:S(2)}) %all-to-all-start) | async-done | bytes 1212448 | tf_op jit(solution)/shard_map/all_to_all | solution.py:290
  25.4 18.1 %half.1 = (f32[296,128]{1,0:T(8,128)S(1)}, f32[11,128,256]{2,1,0:T(8,128)S(1)}, f32[8,16,256]{2,1,0:T(8,128)S(1)}) custom-call(f32[8,296,128]{2,1,0:T(8,128)S(1)} %all-to-all-done.got_ref), custom_call_target="tpu_custom_call" | custom-call | tf_op jit(solution)/shard_map/half/pallas_call | solution.py:274
  43.6 0.0 copy-start.1
  43.6 0.0 copy-start.2
  43.6 9.2 %collective-permute-start = (f32[296,128]{1,0:T(8,128)S(1)}, f32[296,128]{1,0:T(8,128)S(1)}, u32[]{:S(2)}, u32[]{:S(2)}) collective-permute-start(f32[296,128]{1,0:T(8,128)S(1)} %get-tuple-element.5.mine_ref), channel_id=1, source_target_pairs={{0,12},{1,13},{2,14},{3,15},{4,8},{5,9},{6,10},{7,11},{8,4},{9,5},... | collective-permute-start | bytes 454664 | tf_op jit(solution)/shard_map/ppermute | solution.py:294
  52.8 2.5 %collective-permute-done.other_ref = f32[296,128]{1,0:T(8,128)S(1)} collective-permute-done((f32[296,128]{1,0:T(8,128)S(1)}, f32[296,128]{1,0:T(8,128)S(1)}, u32[]{:S(2)}, u32[]{:S(2)}) %collective-permute-start) | collective-permute-done | bytes 151584 | tf_op jit(solution)/shard_map/ppermute | solution.py:294
  55.4 12.7 %middle.1 = f32[8,128]{1,0:T(8,128)} custom-call(f32[296,128]{1,0:T(8,128)S(1)} %get-tuple-element.5.mine_ref, f32[296,128]{1,0:T(8,128)S(1)} %collective-permute-done.other_ref, f32[11,128,256]{2,1,0:T(8,128)S(1)} %get-tuple-element.6.w_ref, f32[8,16,256]{2,1,0:T(8,128)S(1)} %get-tuple-element.7.y_ref), custom_call_target="tpu_custom_call" | custom-call | tf_op jit(solution)/shard_map/middle/pallas_call | solution.py:274
  68.1 3.8 %all-to-all-start.1 = ((f32[8,1,128]{2,1,0:T(1,128)}), f32[8,1,128]{2,1,0:T(1,128)S(1)}, u32[]{:S(2)}, u32[]{:S(2)}) async-start(f32[8,1,128]{2,1,0:T(1,128)} %bitcast.2), calls=%async_computation.1 | async-start | bytes 8192 | tf_op jit(solution)/shard_map/all_to_all | solution.py:296
  71.9 0.0 copy-done.1
  71.9 0.0 copy-done.2
  71.9 0.1 fusion
  72.0 4.9 %all-to-all-done.1 = f32[8,1,128]{2,1,0:T(1,128)S(1)} async-done(((f32[8,1,128]{2,1,0:T(1,128)}), f32[8,1,128]{2,1,0:T(1,128)S(1)}, u32[]{:S(2)}, u32[]{:S(2)}) %all-to-all-start.1) | async-done | bytes 4128 | tf_op jit(solution)/shard_map/all_to_all | solution.py:296
  76.9 0.0 copy-start
  76.9 4.9 %all-gather.2 = f32[2,1,128]{2,1,0:T(1,128)S(1)} all-gather(f32[1,1,128]{2,1,0:T(1,128)S(1)} %bitcast.16), channel_id=2, replica_groups={{0,16},{32,48},{64,80},{96,112},{128,144},{160,176},{192,208},{224,240}..., dimensions={0}, use_global_device_ids=true | all-gather | bytes 1536 | tf_op jit(solution)/shard_map/all_gather | solution.py:310
  81.8 3.8 %collective-permute-start.1 = (f32[2,128]{1,0:T(2,128)S(1)}, f32[2,128]{1,0:T(2,128)S(1)}, u32[]{:S(2)}, u32[]{:S(2)}) collective-permute-start(f32[2,128]{1,0:T(2,128)S(1)} %bitcast.12), channel_id=1, source_target_pairs={{16,48},{32,0},{48,80},{64,32},{80,112},{96,64},{112,144},{128,96}... | collective-permute-start | bytes 3080 | tf_op jit(solution)/shard_map/ppermute | solution.py:308
  85.7 4.9 %collective-permute-start.2 = (f32[2,128]{1,0:T(2,128)S(1)}, f32[2,128]{1,0:T(2,128)S(1)}, u32[]{:S(2)}, u32[]{:S(2)}) collective-permute-start(f32[2,128]{1,0:T(2,128)S(1)} %bitcast.13), channel_id=1, source_target_pairs={{16,80},{48,112},{64,0},{80,144},{96,32},{112,176},{128,64},{144,2... | collective-permute-start | bytes 3080 | tf_op jit(solution)/shard_map/ppermute | solution.py:308
  90.6 0.0 collective-permute-done.1
  90.6 0.7 collective-permute-done.2
  91.3 7.4 %collective-permute-start.3 = (f32[6,128]{1,0:T(8,128)S(1)}, f32[6,128]{1,0:T(8,128)S(1)}, u32[]{:S(2)}, u32[]{:S(2)}) collective-permute-start(f32[6,128]{1,0:T(8,128)S(1)} %pad_maximum_fusion.1), channel_id=1, source_target_pairs={{16,112},{48,144},{80,176},{96,0},{112,208},{128,32},{144,240},{16... | collective-permute-start | bytes 9224 | tf_op jit(solution)/shard_map/ppermute | solution.py:308
  98.8 0.1 copy.12
  98.9 0.6 collective-permute-done.3
  99.5 0.1 multiply_reduce_fusion
  99.6 2.5 %all-gather.3 = f32[2,2,128]{2,1,0:T(2,128)S(1)} all-gather(f32[1,2,128]{2,1,0:T(2,128)S(1)} %bitcast.11), channel_id=3, replica_groups={{0,16},{32,48},{64,80},{96,112},{128,144},{160,176},{192,208},{224,240}..., dimensions={0}, use_global_device_ids=true | all-gather | bytes 3072 | tf_op jit(solution)/shard_map/all_gather | solution.py:322
  102.1 0.5 dynamic-slice_bitcast_fusion
  102.6 0.0 copy-done
  (8 shorter events, 0.1 us)
Async XLA Ops:
  8.3 17.1 %all-to-all-start = ((f32[8,296,128]{2,1,0:T(8,128)}), f32[8,296,128]{2,1,0:T(8,128)S(1)}, u32[]{:S(2)}, u32[]{:S(2)}) async-start(f32[8,296,128]{2,1,0:T(8,128)} %own_inverse.1), calls=%async_computation | async-start | bytes 2424832 | tf_op jit(solution)/shard_map/all_to_all | solution.py:290
  43.6 28.3 %copy-start.1 = (f32[6]{0:T(128)S(1)}, f32[6]{0:T(128)}, u32[]{:S(2)}) copy-start(f32[6]{0:T(128)} %param.14) | copy-start | bytes 76
  43.6 28.3 %copy-start.2 = (s32[6]{0:T(128)S(1)}, s32[6]{0:T(128)}, u32[]{:S(2)}) copy-start(s32[6]{0:T(128)} %param.15) | copy-start | bytes 76
  43.6 11.8 %collective-permute-start = (f32[296,128]{1,0:T(8,128)S(1)}, f32[296,128]{1,0:T(8,128)S(1)}, u32[]{:S(2)}, u32[]{:S(2)}) collective-permute-start(f32[296,128]{1,0:T(8,128)S(1)} %get-tuple-element.5.mine_ref), channel_id=1, source_target_pairs={{0,12},{1,13},{2,14},{3,15},{4,8},{5,9},{6,10},{7,11},{8,4},{9,5},... | collective-permute-start | bytes 454664 | tf_op jit(solution)/shard_map/ppermute | solution.py:294
  68.1 8.8 %all-to-all-start.1 = ((f32[8,1,128]{2,1,0:T(1,128)}), f32[8,1,128]{2,1,0:T(1,128)S(1)}, u32[]{:S(2)}, u32[]{:S(2)}) async-start(f32[8,1,128]{2,1,0:T(1,128)} %bitcast.2), calls=%async_computation.1 | async-start | bytes 8192 | tf_op jit(solution)/shard_map/all_to_all | solution.py:296
  76.9 25.7 %copy-start = (f32[128]{0:T(128)}, f32[128]{0:T(128)S(1)}, u32[]{:S(2)}) copy-start(f32[128]{0:T(128)S(1)} %reduce_sum.27) | copy-start | bytes 1540
  81.8 8.8 %collective-permute-start.1 = (f32[2,128]{1,0:T(2,128)S(1)}, f32[2,128]{1,0:T(2,128)S(1)}, u32[]{:S(2)}, u32[]{:S(2)}) collective-permute-start(f32[2,128]{1,0:T(2,128)S(1)} %bitcast.12), channel_id=1, source_target_pairs={{16,48},{32,0},{48,80},{64,32},{80,112},{96,64},{112,144},{128,96}... | collective-permute-start | bytes 3080 | tf_op jit(solution)/shard_map/ppermute | solution.py:308
  85.7 5.6 %collective-permute-start.2 = (f32[2,128]{1,0:T(2,128)S(1)}, f32[2,128]{1,0:T(2,128)S(1)}, u32[]{:S(2)}, u32[]{:S(2)}) collective-permute-start(f32[2,128]{1,0:T(2,128)S(1)} %bitcast.13), channel_id=1, source_target_pairs={{16,80},{48,112},{64,0},{80,144},{96,32},{112,176},{128,64},{144,2... | collective-permute-start | bytes 3080 | tf_op jit(solution)/shard_map/ppermute | solution.py:308
  91.3 8.2 %collective-permute-start.3 = (f32[6,128]{1,0:T(8,128)S(1)}, f32[6,128]{1,0:T(8,128)S(1)}, u32[]{:S(2)}, u32[]{:S(2)}) collective-permute-start(f32[6,128]{1,0:T(8,128)S(1)} %pad_maximum_fusion.1), channel_id=1, source_target_pairs={{16,112},{48,144},{80,176},{96,0},{112,208},{128,32},{144,240},{16... | collective-permute-start | bytes 9224 | tf_op jit(solution)/shard_map/ppermute | solution.py:308

commit v5 on v2

--- a/solution.py
+++ b/solution.py
@@ -14,6 +14,7 @@
 PACK = N + 8
 broadening = 0.2
 prec = lax.Precision.HIGHEST
+column_prec = lax.Precision.HIGH
 f32 = jnp.float32
 
 GROUPS = [list(range(8)), [12, 13, 14, 15, 8, 9, 10, 11]]
@@ -21,7 +22,8 @@
 
 
 def dot(a, b, dims=((1,), (0,))):
-    return lax.dot_general(a, b, (dims, ((), ())), precision=prec, preferred_element_type=f32)
+    by = column_prec if a.shape[0] == COLS else prec
+    return lax.dot_general(a, b, (dims, ((), ())), precision=by, preferred_element_type=f32)
 
 
 def lanes_of(v, k):
@@ -165,7 +167,7 @@
         out_ref[q, :PACK] = value
 
 
-def half_kernel(got_ref, mid_ref, w_ref, y_ref):
+def half_kernel(got_ref, mid_ref, own_ref, w_ref, y_ref):
     right, _ = sides()
     place = [jnp.bitwise_xor(m, 3 * right) for m in range(HALF)]
     link_place = [jnp.where(right == 1, place[m], m + 1) for m in range(HALF - 1)]
@@ -224,26 +226,52 @@
     keep(w3r)
     D[7] = D[7] - times(flip(V3), w3r)
     z[7] = z[7] + times(z[3], w3r)
-    mid_ref[:PACK] = fold(D[7])
-    mid_ref[PACK : PACK + COLS] = z[7][:, :N]
-    mid_ref[PACK + COLS : PACK + 2 * COLS] = z[7][:, N:]
-    mid_ref[PACK + 2 * COLS :] = got_ref[4, PACK : PACK + N]
-
-
-def middle_kernel(mine_ref, other_ref, w_ref, y_ref, out_ref):
+
+    (q,) = invert([D[7]])
+    own_ref[:N] = D[7]
+    own_ref[N:] = z[7]
+
+    def send(value, row):
+        mid_ref[:PACK] = fold(value)
+        mid_ref[PACK : PACK + COLS] = row[:, :N]
+        mid_ref[PACK + COLS :] = row[:, N:]
+
+    @pl.when(right == 0)
+    def _():
+        send(q, times(z[7], q))
+
+    @pl.when(right == 1)
+    def _():
+        link = got_ref[4, PACK : PACK + N]
+        w = real_times(q, link)
+        send(dot(link.T, w), times(z[7], w))
+
+
+def real_times(a, b):
+    w = dot(jnp.concatenate([a[:, :N], a[:, N:]], axis=0), b)
+    return pack(w[:N], w[N:])
+
+
+def middle_kernel(own_ref, sent_ref, link_ref, w_ref, y_ref, out_ref, block_ref):
     right, _ = sides()
-    link = jnp.where(right == 1, mine_ref[PACK + 2 * COLS :], other_ref[PACK + 2 * COLS :])
-    U = jnp.where(right == 1, link, link.T)
-    UT = jnp.where(right == 1, link.T, link)
-    mine = unfold(mine_ref[:PACK])
-    z = pack(mine_ref[PACK : PACK + COLS], mine_ref[PACK + COLS : PACK + 2 * COLS])
-    z_other = pack(other_ref[PACK : PACK + COLS], other_ref[PACK + COLS : PACK + 2 * COLS])
-    (q,) = invert([unfold(other_ref[:PACK])])
-    w = dot(jnp.concatenate([q[:, :N], q[:, N:]], axis=0), UT)
-    w = pack(w[:N], w[N:])
-    z = z + times(z_other, w)
-    (s,) = invert([mine - dot(U, w)])
-    x = {7: times(z, s)}
+    sent = unfold(sent_ref[:PACK])
+    row = pack(sent_ref[PACK : PACK + COLS], sent_ref[PACK + COLS :])
+
+    @pl.when(right == 0)
+    def _():
+        block_ref[:N] = own_ref[:N] - sent
+        block_ref[N:] = own_ref[N:] + row
+
+    @pl.when(right == 1)
+    def _():
+        link = link_ref[4, PACK : PACK + N]
+        turned_link = link.T
+        block_ref[:N] = own_ref[:N] - dot(link, real_times(sent, turned_link))
+        stacked = dot(jnp.concatenate([row[:, :N], row[:, N:]], axis=0), turned_link)
+        block_ref[N:] = own_ref[N:] + pack(stacked[:COLS], stacked[COLS:])
+
+    (s,) = invert([block_ref[:N]])
+    x = {7: times(block_ref[N:], s)}
     x[3] = y_ref[3] + times_t(x[7], w_ref[10])
     x[5] = y_ref[5] + times_t(x[3], w_ref[8]) + times_t(x[7], w_ref[9])
     x[1] = y_ref[1] + times_t(x[3], w_ref[7])
@@ -256,11 +284,13 @@
         out_ref[jnp.bitwise_xor(m, 3 * right)] = total[0]
 
 
-def call(kernel, shapes, operands, name, streamed=False):
+def call(kernel, shapes, operands, name, streamed=False, scratch=None):
     vmem = pl.BlockSpec(memory_space=pltpu.VMEM)
     many = isinstance(shapes, list)
     extra = {}
     inputs = [vmem] * len(operands)
+    if scratch:
+        extra = dict(scratch_shapes=[pltpu.VMEM(scratch, f32)])
     if streamed:
         inputs = [pl.BlockSpec(memory_space=pltpu.HBM)] * len(operands)
         held = [pltpu.VMEM(v.shape, f32) for v in operands]
@@ -282,11 +312,14 @@
     )
     operands = (energy_level.reshape(1, 1), sigma_real, sigma_width, onsite, coupling, source)
     got = exchange(call(own_kernel, (HALF, PACK + N + 2 * COLS, N), operands, "own_inverse", True))
-    middle, w, y = call(
-        half_kernel, [(PACK + 2 * COLS + N, N), (11, N, 2 * N), (HALF, COLS, 2 * N)], (got,), "half"
+    middle, own, w, y = call(
+        half_kernel,
+        [(PACK + 2 * COLS, N), (N + COLS, 2 * N), (11, N, 2 * N), (HALF, COLS, 2 * N)],
+        (got,),
+        "half",
     )
-    other = lax.ppermute(middle, "transpor", MIRROR)
-    sums = call(middle_kernel, (HALF, N), (middle, other, w, y), "middle")
+    sent = lax.ppermute(middle, "transpor", MIRROR)
+    sums = call(middle_kernel, (HALF, N), (own, sent, got, w, y), "middle", scratch=(N + COLS, 2 * N))
     density = jnp.sum(exchange(sums), axis=0, keepdims=True)
     return (density, mix(density, mode_strength, mode_shift))
 
@@ -302,10 +335,8 @@
         return lax.ppermute(value, "energy", [(a, b) for a, b in steps if 0 <= b < energies])
 
     own = lax.all_gather(density, "energy", axis_index_groups=couples, tiled=True)
-    near = jnp.concatenate([own, fetch(own, 1)], axis=0)
-    middle = fetch(near, 2)
-    far = fetch(middle, 2)
-    window = jnp.concatenate([near, middle, far], axis=0)
+    near = jnp.concatenate([own, fetch(own, 1), fetch(own, 2)], axis=0)
+    window = jnp.concatenate([near, fetch(near, 3)], axis=0)
     row = jnp.arange(window.shape[0], dtype=jnp.int32)
     chip = row // 2
     offset = jnp.where(odd == 1, -chip, chip) * 2 + row % 2

time: 108 us -> 102 us (0.944)
  blocking collectives: 29.1 us -> 7.08 us
  waiting for transfers between devices: 9.36 us -> 19.2 us
  starting transfers between devices: 26.8 us -> 35.2 us
  Pallas kernels: 38.8 us -> 37.1 us
    all_to_all x1 -> x0, blocking collectives: 18.3 us -> none  [on_device(): exchange(call(own_kernel, (HALF, PACK + N + 2 * COLS, N), operands, 'own_...]
    all_to_all x0 -> x1, waiting for transfers between devices: none -> 11.2 us  [on_device(): exchange(call(own_kernel, (HALF, PACK + N + 2 * COLS, N), operands, 'own_...]
    all_to_all x0 -> x1, starting transfers between devices: none -> 5.96 us  [on_device(): exchange(call(own_kernel, (HALF, PACK + N + 2 * COLS, N), operands, 'own_...]
    all_gather x1, blocking collectives: 6.79 us -> 4.59 us  [mix(): lax.all_gather(density, 'energy', axis_index_groups=couples, tiled=True)]
    ppermute x1, starting transfers between devices: 7.57 us -> 9.72 us  [on_device(): sent = lax.ppermute(middle, 'transpor', MIRROR)]
    pallas_call x3, Pallas kernels: 38.8 us -> 37.1 us  [call(): pl.pallas_call(kernel, out_shape=[jax.ShapeDtypeStruct(s, f32) for s in s...]
    all_gather x1, blocking collectives: 3.94 us -> 2.48 us  [mix(): both = lax.all_gather(partial, 'energy', axis_index_groups=couples)]
  transfers between devices with their start and end apart: 5 -> 6, of which waited for: 5 -> 5; matrix products, arithmetic and copies ran while one was open for 0% -> 0% of each run, Pallas kernels for 0% -> 0%
where the time goes in v5:
time: 102 us; the launch traced here: 101 us
  Pallas kernels  37.1 us (36%)
  starting transfers between devices  35.2 us (35%)
  waiting for transfers between devices  19.2 us (19%)
  blocking collectives  7.08 us (7%)
  between operations  1.38 us (1%)
    pallas_call x3, Pallas kernels, call(): pl.pallas_call(kernel, out_shape=[jax.ShapeDtypeStruct(s, f32) for s in s...  37.1 us
    ppermute x3, starting transfers between devices, fetch(): lax.ppermute(value, 'energy', [(a, b) for a, b in steps if 0 <= b < energ...  15.9 us
    all_to_all x1, waiting for transfers between devices, on_device(): exchange(call(own_kernel, (HALF, PACK + N + 2 * COLS, N), operands, 'own_...  11.2 us
    ppermute x1, starting transfers between devices, on_device(): sent = lax.ppermute(middle, 'transpor', MIRROR)  9.72 us
    all_to_all x1, starting transfers between devices, on_device(): exchange(call(own_kernel, (HALF, PACK + N + 2 * COLS, N), operands, 'own_...  5.96 us
    all_to_all x1, waiting for transfers between devices, on_device(): density = jnp.sum(exchange(sums), axis=0, keepdims=True)  4.9 us
    all_gather x1, blocking collectives, mix(): lax.all_gather(density, 'energy', axis_index_groups=couples, tiled=True)  4.59 us
    all_to_all x1, starting transfers between devices, on_device(): density = jnp.sum(exchange(sums), axis=0, keepdims=True)  3.63 us
  transfers between devices with their start and end apart: 6, of which 5 were waited for; matrix products, arithmetic and copies ran while one was open for 0% of the time, Pallas kernels for 0%

profile of v5, /device:TPU:1, one launch (start us, length us, event | category | flops | bytes accessed | tf_op | source)
XLA Modules:
  0.0 100.8 jit_solution(9800047154709634940)
XLA Ops:
  1.3 7.0 %own_inverse.1 = f32[8,296,128]{2,1,0:T(8,128)} custom-call(f32[1,1]{1,0:T(1,128)} %bitcast.10.refs_0_, f32[1,128]{1,0:T(1,128)} %refs_1_.1, f32[1,128]{1,0:T(1,128)} %refs_2_.1, f32[1,128,128]{2,1,0:T(8,128)} %refs_3_.1, f32[1,128,128]{2,1,0:T(8,128)} %refs_4_.1, f32[2,1,1,128,128]{4,3,2,1,0:T(8,128)} %refs_5_.1), custom_call_target="tpu_custom_call" | custom-call | tf_op jit(solution)/shard_map/own_inverse/pallas_call | solution.py:298
  8.3 6.0 %all-to-all-start = ((f32[8,296,128]{2,1,0:T(8,128)}), f32[8,296,128]{2,1,0:T(8,128)S(1)}, u32[]{:S(2)}, u32[]{:S(2)}) async-start(f32[8,296,128]{2,1,0:T(8,128)} %own_inverse.1), calls=%async_computation | async-start | bytes 2424832 | tf_op jit(solution)/shard_map/all_to_all | solution.py:314
  14.3 11.2 %all-to-all-done.got_ref.link_ref = f32[8,296,128]{2,1,0:T(8,128)S(1)} async-done(((f32[8,296,128]{2,1,0:T(8,128)}), f32[8,296,128]{2,1,0:T(8,128)S(1)}, u32[]{:S(2)}, u32[]{:S(2)}) %all-to-all-start) | async-done | bytes 1212448 | tf_op jit(solution)/shard_map/all_to_all | solution.py:314
  25.4 22.5 %half.1 = (f32[168,128]{1,0:T(8,128)S(1)}, f32[144,256]{1,0:T(8,128)S(1)}, f32[11,128,256]{2,1,0:T(8,128)S(1)}, f32[8,16,256]{2,1,0:T(8,128)S(1)}) custom-call(f32[8,296,128]{2,1,0:T(8,128)S(1)} %all-to-all-done.got_ref.link_ref), custom_call_target="tpu_custom_call" | custom-call | tf_op jit(solution)/shard_map/half/pallas_call | solution.py:298
  47.9 9.7 %collective-permute-start = (f32[168,128]{1,0:T(8,128)S(1)}, f32[168,128]{1,0:T(8,128)S(1)}, u32[]{:S(2)}, u32[]{:S(2)}) collective-permute-start(f32[168,128]{1,0:T(8,128)S(1)} %get-tuple-element.7), channel_id=1, source_target_pairs={{0,12},{1,13},{2,14},{3,15},{4,8},{5,9},{6,10},{7,11},{8,4},{9,5},... | collective-permute-start | bytes 258056 | tf_op jit(solution)/shard_map/ppermute | solution.py:321
  57.6 1.8 %collective-permute-done.sent_ref = f32[168,128]{1,0:T(8,128)S(1)} collective-permute-done((f32[168,128]{1,0:T(8,128)S(1)}, f32[168,128]{1,0:T(8,128)S(1)}, u32[]{:S(2)}, u32[]{:S(2)}) %collective-permute-start) | collective-permute-done | bytes 86048 | tf_op jit(solution)/shard_map/ppermute | solution.py:321
  59.5 0.0 copy-start.1
  59.5 0.0 copy-start.2
  59.5 7.6 %middle.1 = f32[8,128]{1,0:T(8,128)} custom-call(f32[144,256]{1,0:T(8,128)S(1)} %get-tuple-element.6.own_ref, f32[168,128]{1,0:T(8,128)S(1)} %collective-permute-done.sent_ref, f32[8,296,128]{2,1,0:T(8,128)S(1)} %all-to-all-done.got_ref.link_ref, f32[11,128,256]{2,1,0:T(8,128)S(1)} %get-tuple-element.8.w_ref, f32[8,16,256]{2,1,0:T(8,128)S(1)} %get-tuple-element.9.y_ref), custom_call_target="tpu_custom_call" | custom-call | tf_op jit(solution)/shard_map/middle/pallas_call | solution.py:298
  67.1 3.6 %all-to-all-start.1 = ((f32[8,1,128]{2,1,0:T(1,128)}), f32[8,1,128]{2,1,0:T(1,128)S(1)}, u32[]{:S(2)}, u32[]{:S(2)}) async-start(f32[8,1,128]{2,1,0:T(1,128)} %bitcast.2), calls=%async_computation.1 | async-start | bytes 8192 | tf_op jit(solution)/shard_map/all_to_all | solution.py:323
  70.7 0.0 copy-done.1
  70.7 0.0 copy-done.2
  70.7 0.1 fusion
  70.8 4.9 %all-to-all-done.1 = f32[8,1,128]{2,1,0:T(1,128)S(1)} async-done(((f32[8,1,128]{2,1,0:T(1,128)}), f32[8,1,128]{2,1,0:T(1,128)S(1)}, u32[]{:S(2)}, u32[]{:S(2)}) %all-to-all-start.1) | async-done | bytes 4128 | tf_op jit(solution)/shard_map/all_to_all | solution.py:323
  75.7 0.0 copy-start
  75.7 4.6 %all-gather.2 = f32[2,1,128]{2,1,0:T(1,128)S(1)} all-gather(f32[1,1,128]{2,1,0:T(1,128)S(1)} %bitcast.16), channel_id=2, replica_groups={{0,16},{32,48},{64,80},{96,112},{128,144},{160,176},{192,208},{224,240}..., dimensions={0}, use_global_device_ids=true | all-gather | bytes 1536 | tf_op jit(solution)/shard_map/all_gather | solution.py:337
  80.3 3.5 %collective-permute-start.1 = (f32[2,128]{1,0:T(2,128)S(1)}, f32[2,128]{1,0:T(2,128)S(1)}, u32[]{:S(2)}, u32[]{:S(2)}) collective-permute-start(f32[2,128]{1,0:T(2,128)S(1)} %bitcast.12), channel_id=1, source_target_pairs={{16,48},{32,0},{48,80},{64,32},{80,112},{96,64},{112,144},{128,96}... | collective-permute-start | bytes 3080 | tf_op jit(solution)/shard_map/ppermute | solution.py:335
  83.9 4.9 %collective-permute-start.2 = (f32[2,128]{1,0:T(2,128)S(1)}, f32[2,128]{1,0:T(2,128)S(1)}, u32[]{:S(2)}, u32[]{:S(2)}) collective-permute-start(f32[2,128]{1,0:T(2,128)S(1)} %bitcast.13), channel_id=1, source_target_pairs={{16,80},{48,112},{64,0},{80,144},{96,32},{112,176},{128,64},{144,2... | collective-permute-start | bytes 3080 | tf_op jit(solution)/shard_map/ppermute | solution.py:335
  88.8 0.0 collective-permute-done.1
  88.8 0.7 collective-permute-done.2
  89.5 7.4 %collective-permute-start.3 = (f32[6,128]{1,0:T(8,128)S(1)}, f32[6,128]{1,0:T(8,128)S(1)}, u32[]{:S(2)}, u32[]{:S(2)}) collective-permute-start(f32[6,128]{1,0:T(8,128)S(1)} %pad_maximum_fusion.1), channel_id=1, source_target_pairs={{16,112},{48,144},{80,176},{96,0},{112,208},{128,32},{144,240},{16... | collective-permute-start | bytes 9224 | tf_op jit(solution)/shard_map/ppermute | solution.py:335
  96.9 0.1 copy.12
  97.0 0.6 collective-permute-done.3
  97.7 0.1 multiply_reduce_fusion
  97.8 2.5 %all-gather.3 = f32[2,2,128]{2,1,0:T(2,128)S(1)} all-gather(f32[1,2,128]{2,1,0:T(2,128)S(1)} %bitcast.11), channel_id=3, replica_groups={{0,16},{32,48},{64,80},{96,112},{128,144},{160,176},{192,208},{224,240}..., dimensions={0}, use_global_device_ids=true | all-gather | bytes 3072 | tf_op jit(solution)/shard_map/all_gather | solution.py:349
  100.3 0.5 dynamic-slice_bitcast_fusion
  100.8 0.0 copy-done
  (8 shorter events, 0.1 us)
Async XLA Ops:
  8.3 17.1 %all-to-all-start = ((f32[8,296,128]{2,1,0:T(8,128)}), f32[8,296,128]{2,1,0:T(8,128)S(1)}, u32[]{:S(2)}, u32[]{:S(2)}) async-start(f32[8,296,128]{2,1,0:T(8,128)} %own_inverse.1), calls=%async_computation | async-start | bytes 2424832 | tf_op jit(solution)/shard_map/all_to_all | solution.py:314
  47.9 11.6 %collective-permute-start = (f32[168,128]{1,0:T(8,128)S(1)}, f32[168,128]{1,0:T(8,128)S(1)}, u32[]{:S(2)}, u32[]{:S(2)}) collective-permute-start(f32[168,128]{1,0:T(8,128)S(1)} %get-tuple-element.7), channel_id=1, source_target_pairs={{0,12},{1,13},{2,14},{3,15},{4,8},{5,9},{6,10},{7,11},{8,4},{9,5},... | collective-permute-start | bytes 258056 | tf_op jit(solution)/shard_map/ppermute | solution.py:321
  59.5 11.2 %copy-start.1 = (f32[6]{0:T(128)S(1)}, f32[6]{0:T(128)}, u32[]{:S(2)}) copy-start(f32[6]{0:T(128)} %param.14) | copy-start | bytes 76
  59.5 11.2 %copy-start.2 = (s32[6]{0:T(128)S(1)}, s32[6]{0:T(128)}, u32[]{:S(2)}) copy-start(s32[6]{0:T(128)} %param.15) | copy-start | bytes 76
  67.1 8.6 %all-to-all-start.1 = ((f32[8,1,128]{2,1,0:T(1,128)}), f32[8,1,128]{2,1,0:T(1,128)S(1)}, u32[]{:S(2)}, u32[]{:S(2)}) async-start(f32[8,1,128]{2,1,0:T(1,128)} %bitcast.2), calls=%async_computation.1 | async-start | bytes 8192 | tf_op jit(solution)/shard_map/all_to_all | solution.py:323
  75.7 25.1 %copy-start = (f32[128]{0:T(128)}, f32[128]{0:T(128)S(1)}, u32[]{:S(2)}) copy-start(f32[128]{0:T(128)S(1)} %reduce_sum.27) | copy-start | bytes 1540
  80.3 8.5 %collective-permute-start.1 = (f32[2,128]{1,0:T(2,128)S(1)}, f32[2,128]{1,0:T(2,128)S(1)}, u32[]{:S(2)}, u32[]{:S(2)}) collective-permute-start(f32[2,128]{1,0:T(2,128)S(1)} %bitcast.12), channel_id=1, source_target_pairs={{16,48},{32,0},{48,80},{64,32},{80,112},{96,64},{112,144},{128,96}... | collective-permute-start | bytes 3080 | tf_op jit(solution)/shard_map/ppermute | solution.py:335
  83.9 5.6 %collective-permute-start.2 = (f32[2,128]{1,0:T(2,128)S(1)}, f32[2,128]{1,0:T(2,128)S(1)}, u32[]{:S(2)}, u32[]{:S(2)}) collective-permute-start(f32[2,128]{1,0:T(2,128)S(1)} %bitcast.13), channel_id=1, source_target_pairs={{16,80},{48,112},{64,0},{80,144},{96,32},{112,176},{128,64},{144,2... | collective-permute-start | bytes 3080 | tf_op jit(solution)/shard_map/ppermute | solution.py:335
  89.5 8.2 %collective-permute-start.3 = (f32[6,128]{1,0:T(8,128)S(1)}, f32[6,128]{1,0:T(8,128)S(1)}, u32[]{:S(2)}, u32[]{:S(2)}) collective-permute-start(f32[6,128]{1,0:T(8,128)S(1)} %pad_maximum_fusion.1), channel_id=1, source_target_pairs={{16,112},{48,144},{80,176},{96,0},{112,208},{128,32},{144,240},{16... | collective-permute-start | bytes 9224 | tf_op jit(solution)/shard_map/ppermute | solution.py:335

commit v6 on v5

--- a/solution.py
+++ b/solution.py
@@ -21,8 +21,8 @@
 MIRROR = [(x * 4 + y, (3 - x) * 4 + y) for x in range(4) for y in range(4)]
 
 
-def dot(a, b, dims=((1,), (0,))):
-    by = column_prec if a.shape[0] == COLS else prec
+def dot(a, b, dims=((1,), (0,)), exact=False):
+    by = column_prec if a.shape[0] == COLS and not exact else prec
     return lax.dot_general(a, b, (dims, ((), ())), precision=by, preferred_element_type=f32)
 
 
@@ -63,9 +63,12 @@
     return lax.broadcasted_iota(jnp.int32, shape, d)
 
 
-def invert(ms, ahead=2):
+def invert(ms, ahead=2, rows=None):
     R = [[m[8 * u : 8 * u + 8, :N] for u in range(TILES)] for m in ms]
     I = [[m[8 * u : 8 * u + 8, N:] for u in range(TILES)] for m in ms]
+    if rows is not None:
+        R[0] += [rows[8 * q : 8 * q + 8, :N] for q in range(COLS // 8)]
+        I[0] += [rows[8 * q : 8 * q + 8, N:] for q in range(COLS // 8)]
     sub, lane = iota((8, N), 0), iota((8, N), 1)
     zero = jnp.zeros((8, 2 * N), f32)
     for t in range(TILES):
@@ -104,18 +107,20 @@
                     yr = yr - lr[u][j] * br + li[u][j] * bi
                     yi = yi - lr[u][j] * bi - li[u][j] * br
                 new[u] = (yr, yi)
-            rest = [u for u in range(TILES) if u not in new]
+            rest = [u for u in range(len(xr)) if u not in new and (rows is None or u > t)]
             left = jnp.concatenate([pack(xr[u], xi[u]) for u in rest], 0)
             top = [pack(pr, pi) if u == t else zero for u in range(TILES)]
             low = [pack(-pi, pr) if u == t else zero for u in range(TILES)]
-            delta = dot(left, jnp.concatenate(top + low, 0))
+            delta = dot(left, jnp.concatenate(top + low, 0), exact=True)
             for q, u in enumerate(rest):
                 new[u] = (
                     jnp.where(here, 0.0, xr[u]) - delta[8 * q : 8 * q + 8, :N],
                     jnp.where(here, 0.0, xi[u]) - delta[8 * q : 8 * q + 8, N:],
                 )
-            R[b] = [new[u][0] for u in range(TILES)]
-            I[b] = [new[u][1] for u in range(TILES)]
+            R[b] = [new[u][0] if u in new else xr[u] for u in range(len(xr))]
+            I[b] = [new[u][1] if u in new else xi[u] for u in range(len(xi))]
+    if rows is not None:
+        return jnp.concatenate([pack(-r, -i) for r, i in zip(R[0][TILES:], I[0][TILES:])], 0)
     return [jnp.concatenate([pack(r, i) for r, i in zip(R[b], I[b])], 0) for b in range(len(ms))]
 
 
@@ -270,8 +275,7 @@
         stacked = dot(jnp.concatenate([row[:, :N], row[:, N:]], axis=0), turned_link)
         block_ref[N:] = own_ref[N:] + pack(stacked[:COLS], stacked[COLS:])
 
-    (s,) = invert([block_ref[:N]])
-    x = {7: times(block_ref[N:], s)}
+    x = {7: invert([block_ref[:N]], rows=block_ref[N:])}
     x[3] = y_ref[3] + times_t(x[7], w_ref[10])
     x[5] = y_ref[5] + times_t(x[3], w_ref[8]) + times_t(x[7], w_ref[9])
     x[1] = y_ref[1] + times_t(x[3], w_ref[7])

time: 102 us -> 102 us (level)
  no operation moved by 1% of the time
where the time goes in v6:
time: 102 us; the launch traced here: 100 us
  Pallas kernels  36.7 us (36%)
  starting transfers between devices  35.2 us (35%)
  waiting for transfers between devices  19.2 us (19%)
  blocking collectives  7.08 us (7%)
  between operations  1.38 us (1%)
    pallas_call x3, Pallas kernels, call(): pl.pallas_call(kernel, out_shape=[jax.ShapeDtypeStruct(s, f32) for s in s...  36.7 us
    ppermute x3, starting transfers between devices, fetch(): lax.ppermute(value, 'energy', [(a, b) for a, b in steps if 0 <= b < energ...  15.9 us
    all_to_all x1, waiting for transfers between devices, on_device(): exchange(call(own_kernel, (HALF, PACK + N + 2 * COLS, N), operands, 'own_...  11.2 us
    ppermute x1, starting transfers between devices, on_device(): sent = lax.ppermute(middle, 'transpor', MIRROR)  9.72 us
    all_to_all x1, starting transfers between devices, on_device(): exchange(call(own_kernel, (HALF, PACK + N + 2 * COLS, N), operands, 'own_...  5.96 us
    all_to_all x1, waiting for transfers between devices, on_device(): density = jnp.sum(exchange(sums), axis=0, keepdims=True)  4.9 us
    all_gather x1, blocking collectives, mix(): lax.all_gather(density, 'energy', axis_index_groups=couples, tiled=True)  4.59 us
    all_to_all x1, starting transfers between devices, on_device(): density = jnp.sum(exchange(sums), axis=0, keepdims=True)  3.63 us
  transfers between devices with their start and end apart: 6, of which 5 were waited for; matrix products, arithmetic and copies ran while one was open for 0% of the time, Pallas kernels for 0%

profile of v6, /device:TPU:1, one launch (start us, length us, event | category | flops | bytes accessed | tf_op | source)
XLA Modules:
  0.0 100.4 jit_solution(4987981986804879109)
XLA Ops:
  1.3 7.0 %own_inverse.1 = f32[8,296,128]{2,1,0:T(8,128)} custom-call(f32[1,1]{1,0:T(1,128)} %bitcast.10.refs_0_, f32[1,128]{1,0:T(1,128)} %refs_1_.1, f32[1,128]{1,0:T(1,128)} %refs_2_.1, f32[1,128,128]{2,1,0:T(8,128)} %refs_3_.1, f32[1,128,128]{2,1,0:T(8,128)} %refs_4_.1, f32[2,1,1,128,128]{4,3,2,1,0:T(8,128)} %refs_5_.1), custom_call_target="tpu_custom_call" | custom-call | tf_op jit(solution)/shard_map/own_inverse/pallas_call | solution.py:302
  8.3 6.0 %all-to-all-start = ((f32[8,296,128]{2,1,0:T(8,128)}), f32[8,296,128]{2,1,0:T(8,128)S(1)}, u32[]{:S(2)}, u32[]{:S(2)}) async-start(f32[8,296,128]{2,1,0:T(8,128)} %own_inverse.1), calls=%async_computation | async-start | bytes 2424832 | tf_op jit(solution)/shard_map/all_to_all | solution.py:318
  14.3 11.2 %all-to-all-done.got_ref.link_ref = f32[8,296,128]{2,1,0:T(8,128)S(1)} async-done(((f32[8,296,128]{2,1,0:T(8,128)}), f32[8,296,128]{2,1,0:T(8,128)S(1)}, u32[]{:S(2)}, u32[]{:S(2)}) %all-to-all-start) | async-done | bytes 1212448 | tf_op jit(solution)/shard_map/all_to_all | solution.py:318
  25.4 22.5 %half.1 = (f32[168,128]{1,0:T(8,128)S(1)}, f32[144,256]{1,0:T(8,128)S(1)}, f32[11,128,256]{2,1,0:T(8,128)S(1)}, f32[8,16,256]{2,1,0:T(8,128)S(1)}) custom-call(f32[8,296,128]{2,1,0:T(8,128)S(1)} %all-to-all-done.got_ref.link_ref), custom_call_target="tpu_custom_call" | custom-call | tf_op jit(solution)/shard_map/half/pallas_call | solution.py:302
  47.9 9.7 %collective-permute-start = (f32[168,128]{1,0:T(8,128)S(1)}, f32[168,128]{1,0:T(8,128)S(1)}, u32[]{:S(2)}, u32[]{:S(2)}) collective-permute-start(f32[168,128]{1,0:T(8,128)S(1)} %get-tuple-element.7), channel_id=1, source_target_pairs={{0,12},{1,13},{2,14},{3,15},{4,8},{5,9},{6,10},{7,11},{8,4},{9,5},... | collective-permute-start | bytes 258056 | tf_op jit(solution)/shard_map/ppermute | solution.py:325
  57.6 1.8 %collective-permute-done.sent_ref = f32[168,128]{1,0:T(8,128)S(1)} collective-permute-done((f32[168,128]{1,0:T(8,128)S(1)}, f32[168,128]{1,0:T(8,128)S(1)}, u32[]{:S(2)}, u32[]{:S(2)}) %collective-permute-start) | collective-permute-done | bytes 86048 | tf_op jit(solution)/shard_map/ppermute | solution.py:325
  59.5 0.0 copy-start.1
  59.5 0.0 copy-start.2
  59.5 7.2 %middle.1 = f32[8,128]{1,0:T(8,128)} custom-call(f32[144,256]{1,0:T(8,128)S(1)} %get-tuple-element.6.own_ref, f32[168,128]{1,0:T(8,128)S(1)} %collective-permute-done.sent_ref, f32[8,296,128]{2,1,0:T(8,128)S(1)} %all-to-all-done.got_ref.link_ref, f32[11,128,256]{2,1,0:T(8,128)S(1)} %get-tuple-element.8.w_ref, f32[8,16,256]{2,1,0:T(8,128)S(1)} %get-tuple-element.9.y_ref), custom_call_target="tpu_custom_call" | custom-call | tf_op jit(solution)/shard_map/middle/pallas_call | solution.py:302
  66.7 3.6 %all-to-all-start.1 = ((f32[8,1,128]{2,1,0:T(1,128)}), f32[8,1,128]{2,1,0:T(1,128)S(1)}, u32[]{:S(2)}, u32[]{:S(2)}) async-start(f32[8,1,128]{2,1,0:T(1,128)} %bitcast.2), calls=%async_computation.1 | async-start | bytes 8192 | tf_op jit(solution)/shard_map/all_to_all | solution.py:327
  70.3 0.0 copy-done.1
  70.3 0.0 copy-done.2
  70.3 0.1 fusion
  70.4 4.9 %all-to-all-done.1 = f32[8,1,128]{2,1,0:T(1,128)S(1)} async-done(((f32[8,1,128]{2,1,0:T(1,128)}), f32[8,1,128]{2,1,0:T(1,128)S(1)}, u32[]{:S(2)}, u32[]{:S(2)}) %all-to-all-start.1) | async-done | bytes 4128 | tf_op jit(solution)/shard_map/all_to_all | solution.py:327
  75.3 0.0 copy-start
  75.3 4.6 %all-gather.2 = f32[2,1,128]{2,1,0:T(1,128)S(1)} all-gather(f32[1,1,128]{2,1,0:T(1,128)S(1)} %bitcast.16), channel_id=2, replica_groups={{0,16},{32,48},{64,80},{96,112},{128,144},{160,176},{192,208},{224,240}..., dimensions={0}, use_global_device_ids=true | all-gather | bytes 1536 | tf_op jit(solution)/shard_map/all_gather | solution.py:341
  79.9 3.5 %collective-permute-start.1 = (f32[2,128]{1,0:T(2,128)S(1)}, f32[2,128]{1,0:T(2,128)S(1)}, u32[]{:S(2)}, u32[]{:S(2)}) collective-permute-start(f32[2,128]{1,0:T(2,128)S(1)} %bitcast.12), channel_id=1, source_target_pairs={{16,48},{32,0},{48,80},{64,32},{80,112},{96,64},{112,144},{128,96}... | collective-permute-start | bytes 3080 | tf_op jit(solution)/shard_map/ppermute | solution.py:339
  83.5 4.9 %collective-permute-start.2 = (f32[2,128]{1,0:T(2,128)S(1)}, f32[2,128]{1,0:T(2,128)S(1)}, u32[]{:S(2)}, u32[]{:S(2)}) collective-permute-start(f32[2,128]{1,0:T(2,128)S(1)} %bitcast.13), channel_id=1, source_target_pairs={{16,80},{48,112},{64,0},{80,144},{96,32},{112,176},{128,64},{144,2... | collective-permute-start | bytes 3080 | tf_op jit(solution)/shard_map/ppermute | solution.py:339
  88.4 0.0 collective-permute-done.1
  88.4 0.7 collective-permute-done.2
  89.1 7.4 %collective-permute-start.3 = (f32[6,128]{1,0:T(8,128)S(1)}, f32[6,128]{1,0:T(8,128)S(1)}, u32[]{:S(2)}, u32[]{:S(2)}) collective-permute-start(f32[6,128]{1,0:T(8,128)S(1)} %pad_maximum_fusion.1), channel_id=1, source_target_pairs={{16,112},{48,144},{80,176},{96,0},{112,208},{128,32},{144,240},{16... | collective-permute-start | bytes 9224 | tf_op jit(solution)/shard_map/ppermute | solution.py:339
  96.5 0.1 copy.12
  96.6 0.6 collective-permute-done.3
  97.3 0.1 multiply_reduce_fusion
  97.4 2.5 %all-gather.3 = f32[2,2,128]{2,1,0:T(2,128)S(1)} all-gather(f32[1,2,128]{2,1,0:T(2,128)S(1)} %bitcast.11), channel_id=3, replica_groups={{0,16},{32,48},{64,80},{96,112},{128,144},{160,176},{192,208},{224,240}..., dimensions={0}, use_global_device_ids=true | all-gather | bytes 3072 | tf_op jit(solution)/shard_map/all_gather | solution.py:353
  99.9 0.5 dynamic-slice_bitcast_fusion
  100.4 0.0 copy-done
  (8 shorter events, 0.1 us)
Async XLA Ops:
  8.3 17.1 %all-to-all-start = ((f32[8,296,128]{2,1,0:T(8,128)}), f32[8,296,128]{2,1,0:T(8,128)S(1)}, u32[]{:S(2)}, u32[]{:S(2)}) async-start(f32[8,296,128]{2,1,0:T(8,128)} %own_inverse.1), calls=%async_computation | async-start | bytes 2424832 | tf_op jit(solution)/shard_map/all_to_all | solution.py:318
  47.9 11.6 %collective-permute-start = (f32[168,128]{1,0:T(8,128)S(1)}, f32[168,128]{1,0:T(8,128)S(1)}, u32[]{:S(2)}, u32[]{:S(2)}) collective-permute-start(f32[168,128]{1,0:T(8,128)S(1)} %get-tuple-element.7), channel_id=1, source_target_pairs={{0,12},{1,13},{2,14},{3,15},{4,8},{5,9},{6,10},{7,11},{8,4},{9,5},... | collective-permute-start | bytes 258056 | tf_op jit(solution)/shard_map/ppermute | solution.py:325
  59.5 10.8 %copy-start.1 = (f32[6]{0:T(128)S(1)}, f32[6]{0:T(128)}, u32[]{:S(2)}) copy-start(f32[6]{0:T(128)} %param.14) | copy-start | bytes 76
  59.5 10.8 %copy-start.2 = (s32[6]{0:T(128)S(1)}, s32[6]{0:T(128)}, u32[]{:S(2)}) copy-start(s32[6]{0:T(128)} %param.15) | copy-start | bytes 76
  66.7 8.6 %all-to-all-start.1 = ((f32[8,1,128]{2,1,0:T(1,128)}), f32[8,1,128]{2,1,0:T(1,128)S(1)}, u32[]{:S(2)}, u32[]{:S(2)}) async-start(f32[8,1,128]{2,1,0:T(1,128)} %bitcast.2), calls=%async_computation.1 | async-start | bytes 8192 | tf_op jit(solution)/shard_map/all_to_all | solution.py:327
  75.3 25.1 %copy-start = (f32[128]{0:T(128)}, f32[128]{0:T(128)S(1)}, u32[]{:S(2)}) copy-start(f32[128]{0:T(128)S(1)} %reduce_sum.27) | copy-start | bytes 1540
  79.9 8.5 %collective-permute-start.1 = (f32[2,128]{1,0:T(2,128)S(1)}, f32[2,128]{1,0:T(2,128)S(1)}, u32[]{:S(2)}, u32[]{:S(2)}) collective-permute-start(f32[2,128]{1,0:T(2,128)S(1)} %bitcast.12), channel_id=1, source_target_pairs={{16,48},{32,0},{48,80},{64,32},{80,112},{96,64},{112,144},{128,96}... | collective-permute-start | bytes 3080 | tf_op jit(solution)/shard_map/ppermute | solution.py:339
  83.5 5.6 %collective-permute-start.2 = (f32[2,128]{1,0:T(2,128)S(1)}, f32[2,128]{1,0:T(2,128)S(1)}, u32[]{:S(2)}, u32[]{:S(2)}) collective-permute-start(f32[2,128]{1,0:T(2,128)S(1)} %bitcast.13), channel_id=1, source_target_pairs={{16,80},{48,112},{64,0},{80,144},{96,32},{112,176},{128,64},{144,2... | collective-permute-start | bytes 3080 | tf_op jit(solution)/shard_map/ppermute | solution.py:339
  89.1 8.2 %collective-permute-start.3 = (f32[6,128]{1,0:T(8,128)S(1)}, f32[6,128]{1,0:T(8,128)S(1)}, u32[]{:S(2)}, u32[]{:S(2)}) collective-permute-start(f32[6,128]{1,0:T(8,128)S(1)} %pad_maximum_fusion.1), channel_id=1, source_target_pairs={{16,112},{48,144},{80,176},{96,0},{112,208},{128,32},{144,240},{16... | collective-permute-start | bytes 9224 | tf_op jit(solution)/shard_map/ppermute | solution.py:339
